TPU v7x, 32 devices: a whole 2x2x4 slice. The times are simulated.
32 devices in a mesh: seq: 8 (over z, x), head: 4 (over y, core).
Axes of the slice: x: 2, y: 2, z: 4, core: 2. Of those that a mesh axis runs over, the one named last changes fastest.
Arguments:
- inner_input: bfloat16 [4096, 16384], P('seq', 'head'), may hold values from -6 to 6
- state_input: bfloat16 [4096, 4096], P('seq', 'head'), may hold values from -6 to 6
- gate_input: bfloat16 [4096, 16384], P('seq', 'head'), may hold values from -6 to 6
- inner_taps: bfloat16 [4, 16384], P(None, 'head'), may hold values from -3 to 3
- inner_bias: bfloat16 [16384], P('head'), may hold values from -3 to 3
- state_taps: bfloat16 [4, 4096], P(None, 'head'), may hold values from -3 to 3
- state_bias: bfloat16 [4096], P('head'), may hold values from -3 to 3
- step_raw: float32 [256, 4096], P('head', 'seq'), may hold values from -5.3 to -1
- step_bias: float32 [256], P('head'), may hold values from -0.5 to 0.5
- decay_log: float32 [256], P('head'), may hold values from -9 to 1.26
- skip_gain: float32 [256], P('head'), may hold values from 0.5 to 1.5
- norm_gain: bfloat16 [16384], P('head'), may hold values from 0.5 to 1.5
- out_weight: bfloat16 [16384, 4096], P('head', 'seq'), may hold values from -0.0625 to 0.0625
- sequence_lengths: int32 [4], replicated, may hold values from 1 to 2048, 4096 in all
Outputs:
- mixed_out: bfloat16 [4096, 4096], P('seq', 'head')
Inputs may be any that keep to these rules, and one draw needn't show every extreme that they name: `sequence_lengths`: the 4 sequences lie end to end in the order given and fill all 4096 positions; the longest has exactly 2048 positions.
All inputs are finite; a program needn't handle non-finite values.
Results may differ from a plain program's by a relative error of at most 0.018.
Values may be sent and summed in bfloat16 or wider, within the bound.
A program may use at most 256 MiB of HBM per device.

v0:
```python
from functools import partial

import jax
import jax.numpy as jnp
from jax import lax
from jax.sharding import PartitionSpec as P

HEAD_DIM = 64
STATE_DIM = 256
BLOCK_LEN = 256


HIGHEST = lax.Precision.HIGHEST
EPSILON = 1e-05


def passed_along(value, axis, steps):
    count = lax.axis_size(axis)
    initial, last = (max(0, -steps), min(count, count - steps))
    return lax.ppermute(value, axis, [(source, source + steps) for source in range(initial, last)])


def prefix(array, axis, join, neutral):
    place = lax.axis_index(axis)
    gathered = jax.tree.map(
        lambda a, kind: lax.all_gather(a.astype(kind), axis), array, (jnp.bfloat16, jnp.bfloat16)
    )
    state = jax.tree.map(lambda a, e: jnp.zeros_like(a) + jnp.asarray(e, a.dtype), array, neutral)

    def one(step, state):
        return join(
            state,
            jax.tree.map(
                lambda a, own: lax.dynamic_index_in_dim(a, step, 0, False).astype(own.dtype),
                gathered,
                array,
            ),
        )

    return lax.fori_loop(0, place, one, state)


def segment_of(positions, sequence_lengths):
    starts = jnp.cumsum(sequence_lengths) - sequence_lengths
    hits = (positions[:, None] >= starts[None, :]).astype(jnp.int32)
    return jnp.sum(hits, axis=1) - 1


def causal_conv(extended, seg_extended, tap_table, bias_row):
    tap_count = tap_table.shape[0]
    length = extended.shape[0] - tap_count + 1
    current = seg_extended[tap_count - 1 :]
    summed = jnp.zeros((length, bias_row.shape[0]), jnp.float32) + bias_row.astype(jnp.float32)
    for start_shift in range(tap_count):
        kept_mask = (seg_extended[start_shift : start_shift + length] == current).astype(
            jnp.float32
        )
        summed = (
            summed
            + tap_table[start_shift].astype(jnp.float32)
            * extended[start_shift : start_shift + length].astype(jnp.float32)
            * kept_mask[:, None]
        )
    return jax.nn.silu(summed).astype(jnp.bfloat16)


def block_step(decay_rates, skip_gains, carried, inputs):
    state_now, seg_before = carried
    input_block, write_block, read_block, step_block, seg_block = inputs
    block_rows = input_block.shape[0]
    log_decay = -decay_rates[..., None] * step_block
    running = jnp.cumsum(log_decay, axis=2)
    input_vals = input_block.astype(jnp.float32)
    write_vecs = write_block.astype(jnp.float32)
    read_vecs = read_block.astype(jnp.float32)
    scores = jnp.einsum("ign,jgn->gij", read_vecs, write_vecs, precision=HIGHEST)
    row_index = lax.broadcasted_iota(jnp.int32, (block_rows, block_rows), 0)
    col_index = lax.broadcasted_iota(jnp.int32, (block_rows, block_rows), 1)
    linked = (row_index >= col_index) & (seg_block[:, None] == seg_block[None, :])
    spread = running[..., :, None] - running[..., None, :]
    decays = jnp.where(linked, jnp.exp(jnp.where(linked, spread, 0.0)), 0.0)
    scaled = input_vals * jnp.transpose(step_block, (2, 0, 1))[..., None]
    within = jnp.einsum("ghij,jghp->ighp", decays * scores[:, None], scaled, precision=HIGHEST)
    alive_mask = (seg_block == seg_before).astype(jnp.float32)
    entering = jnp.transpose(alive_mask * jnp.exp(running), (2, 0, 1))
    carried_out = (
        jnp.einsum("ign,ghpn->ighp", read_vecs, state_now, precision=HIGHEST) * entering[..., None]
    )
    outputs = within + carried_out + skip_gains[..., None] * input_vals
    last_seg = seg_block[block_rows - 1]
    closing = (seg_block == last_seg).astype(jnp.float32) * jnp.exp(
        running[..., block_rows - 1 :] - running
    )
    weighted = scaled * jnp.transpose(closing, (2, 0, 1))[..., None]
    kept = (alive_mask[block_rows - 1] * jnp.exp(running[..., block_rows - 1]))[..., None, None]
    new_state = kept * state_now + jnp.einsum(
        "jghp,jgn->ghpn", weighted, write_vecs, precision=HIGHEST
    )
    return ((new_state, last_seg), outputs)


def join_states(earlier, later):
    return (earlier[0] * later[0], later[0][..., None, None] * earlier[1] + later[1])


def per_device(
    inner_input,
    state_input,
    gate_input,
    inner_taps,
    inner_bias,
    state_taps,
    state_bias,
    step_raw,
    step_bias,
    decay_log,
    skip_gain,
    norm_gain,
    out_weight,
    sequence_lengths,
):
    tok_rows = inner_input.shape[0]
    inner_width = inner_input.shape[1]
    head_local = step_raw.shape[0]
    group_local = state_input.shape[1] // (2 * STATE_DIM)
    per_group = head_local // group_local
    tap_count = inner_taps.shape[0]
    block_count = tok_rows // BLOCK_LEN
    first_row = lax.axis_index("seq") * tok_rows
    positions = first_row + lax.iota(jnp.int32, tok_rows + tap_count - 1) - (tap_count - 1)
    seg_extended = segment_of(positions, sequence_lengths)
    seg_local = seg_extended[tap_count - 1 :]
    seg_before = seg_extended[tap_count - 2]
    tail_rows = jnp.concatenate(
        [inner_input[tok_rows - tap_count + 1 :], state_input[tok_rows - tap_count + 1 :]], axis=1
    )
    received = passed_along(tail_rows, "seq", 1)
    inner_conv = causal_conv(
        jnp.concatenate([received[:, :inner_width], inner_input]),
        seg_extended,
        inner_taps,
        inner_bias,
    )
    state_conv = causal_conv(
        jnp.concatenate([received[:, inner_width:], state_input]),
        seg_extended,
        state_taps,
        state_bias,
    )
    inputs_all = inner_conv.reshape(tok_rows, group_local, per_group, HEAD_DIM)
    vectors = state_conv.reshape(tok_rows, group_local, 2, STATE_DIM)
    write_all = vectors[:, :, 0]
    read_all = vectors[:, :, 1]
    steps_all = jax.nn.softplus(step_raw + step_bias[:, None]).reshape(
        group_local, per_group, tok_rows
    )
    decay_rates = jnp.exp(decay_log).reshape(group_local, per_group)
    skip_gains = skip_gain.reshape(group_local, per_group)
    running = jnp.cumsum(-decay_rates[..., None] * steps_all, axis=2)
    alive_mask = (seg_local == seg_before).astype(jnp.float32)
    factor = alive_mask[tok_rows - 1] * jnp.exp(running[..., tok_rows - 1])
    sequence = (
        inputs_all.reshape(block_count, BLOCK_LEN, group_local, per_group, HEAD_DIM),
        write_all.reshape(block_count, BLOCK_LEN, group_local, STATE_DIM),
        read_all.reshape(block_count, BLOCK_LEN, group_local, STATE_DIM),
        jnp.transpose(
            steps_all.reshape(group_local, per_group, block_count, BLOCK_LEN), (2, 0, 1, 3)
        ),
        seg_local.reshape(block_count, BLOCK_LEN),
    )
    stepper = partial(block_step, decay_rates, skip_gains)
    closing = (seg_local == seg_local[tok_rows - 1]).astype(jnp.float32) * jnp.exp(
        running[..., tok_rows - 1 :] - running
    )
    weighted = (
        inputs_all.astype(jnp.float32) * jnp.transpose(steps_all * closing, (2, 0, 1))[..., None]
    )
    local_state = jnp.einsum(
        "tghp,tgn->ghpn", weighted, write_all.astype(jnp.float32), precision=HIGHEST
    )
    factor_in, state_in = prefix(
        (factor, local_state),
        "seq",
        join_states,
        (jnp.ones_like(factor), jnp.zeros_like(local_state)),
    )
    _, outputs = lax.scan(stepper, (state_in, seg_before), sequence)
    y_all = outputs.reshape(tok_rows, group_local, per_group * HEAD_DIM)
    gated = y_all * jax.nn.silu(gate_input.astype(jnp.float32)).reshape(
        tok_rows, group_local, per_group * HEAD_DIM
    )
    mean_sq = jnp.mean(gated * gated, axis=2, keepdims=True)
    gain_rows = norm_gain.astype(jnp.float32).reshape(group_local, per_group * HEAD_DIM)
    normed = (
        (gated * lax.rsqrt(mean_sq + EPSILON) * gain_rows)
        .astype(jnp.bfloat16)
        .reshape(tok_rows, inner_width)
    )
    partial_out = jnp.dot(
        normed,
        lax.all_gather(out_weight, "seq", axis=1, tiled=True),
        preferred_element_type=jnp.float32,
    )
    return lax.psum_scatter(
        partial_out.astype(jnp.bfloat16), "head", scatter_dimension=1, tiled=True
    )


def solution(mesh):
    in_specs = (
        P("seq", "head"),
        P("seq", "head"),
        P("seq", "head"),
        P(None, "head"),
        P("head"),
        P(None, "head"),
        P("head"),
        P("head", "seq"),
        P("head"),
        P("head"),
        P("head"),
        P("head"),
        P("head", "seq"),
        P(),
    )
    out_specs = P("seq", "head")
    return jax.shard_map(
        per_device, mesh=mesh, in_specs=in_specs, out_specs=out_specs, check_vma=False
    )
```

profile of v0, /device:TPU:24, one launch (start us, length us, event | category | flops | bytes accessed | tf_op | source)
XLA Modules:
  0.0 993.8 jit_solution(2354620652247380052)
XLA Ops:
  6.5 0.9 slice.134
  7.4 0.7 slice.135
  8.2 3.4 collective-permute-start
  11.6 0.8 reduce-window.33
  12.4 0.7 bitcast_subtract_fusion
  13.2 0.6 fusion.62
  13.8 1.0 slice_convert_fusion.3
  14.7 1.1 compare_select_fusion
  15.8 0.7 exponential_negate_fusion
  16.7 2.3 reduce-window.34
  19.5 1.3 compare_convert_fusion.2
  21.0 0.9 slice_convert_fusion.7
  21.9 6.6 copy.106
  28.5 0.5 copy.109
  29.1 0.5 copy.105
  29.8 15.2 %multiply_convert_fusion = bf16[512,4096]{0,1:T(8,128)(2,1)S(1)} fusion(bf16[512,4096]{0,1:T(8,128)(2,1)} %copy.106, bf16[3,4096]{0,1:T(8,128)(2,1)S(1)} %copy.105, f32[4096]{0:T(1024)S(1)} %bitcast.200, f32[512]{0:T(512)S(1)} %get-tuple-element.292, f32[4096]{0:T(1024)S(1)} %bitcast.201, f32[512]{0:T(512)S(1)} %get-tuple-element.293, ...), kind=kLoop, calls=%fused_computation.70 | loop fusion | flops 60817408 | bytes 8501248 | tf_op jit(solution)/shard_map/convert_element_type | solution.py:64
  45.0 2.8 multiply_convert_fusion.1
  47.9 5.6 fusion.53
  53.6 0.7 all-gather.5.cloned.1.call-update
  54.6 0.6 slice.129
  55.8 16.2 %all-gather = bf16[16,32,1]{1,2,0:T(2,128)(2,1)S(1)} all-gather(bf16[2,32,1]{1,2,0:T(2,128)(2,1)S(1)} %copy.104), channel_id=2, replica_groups=mesh['seq'=8,'head'=4] {'seq'}, dimensions={0}, use_global_device_ids=true | all-gather | bytes 1152 | tf_op jit(solution)/shard_map/all_gather | solution.py:26
  72.1 6.5 copy.117
  78.6 5.9 convert_multiply_fusion.5
  84.5 10.6 %reshape.238 = f32[2,256,2,32,64]{1,0,4,3,2:T(2,128)} reshape(f32[512,4096]{0,1:T(8,128)} %convert_multiply_fusion.5) | data formatting | bytes 16777216 | tf_op jit(solution)/shard_map/reshape | solution.py:189
  95.1 0.6 convert_element_type.182
  95.7 7.0 reshape_reshape.7
  103.5 5.1 copy.113
  108.6 170.9 %all-gather.7.cloned.1.call-done = bf16[16,32,64,256]{3,2,1,0:T(8,128)(2,1)} async-done(((bf16[2,32,64,256]{3,2,1,0:T(8,128)(2,1)}), bf16[16,32,64,256]{3,2,1,0:T(8,128)(2,1)}) %all-gather.7.cloned.1.call-update) | async-done | bytes 16777232 | tf_op jit(solution)/shard_map/all_gather | solution.py:26
  279.4 2.4 broadcast_in_dim.22
  281.9 32.3 %while.28 = (s32[]{:T(128)}, f32[2,32,64,256]{3,2,1,0:T(8,128)}, s32[]{:T(128)}, bf16[8,2,32]{2,1,0:T(2,128)(2,1)S(1)}, bf16[8,2,32,64,256]{4,3,2,1,0:T(8,128)(2,1)}, /*index=5*/s32[]{:T(128)}, s32[]{:T(128)}, s32[]{:T(128)}) while((s32[]{:T(128)}, f32[2,32,64,256]{3,2,1,0:T(8,128)}, s32[]{:T(128)}, bf16[8,2,32]{2,1,0:T(2,128)(2,1)S(1)}, ...), condition=%wide.region_5.6_spmd, body=%wide.region_4.5_spmd.sunk | while | flops 3145797 | bytes 10486527 | solution.py:40
  281.9 5.3 convert_add_fusion.2
  287.2 5.9 convert_add_fusion.2
  293.0 5.3 convert_add_fusion.2
  298.3 5.3 convert_add_fusion.2
  303.6 5.3 convert_add_fusion.2
  308.9 5.3 convert_add_fusion.2
  314.2 263.6 %while.29 = (s32[]{:T(128)}, f32[2,32,64,256]{3,2,1,0:T(8,128)}, s32[]{:T(128)}, f32[2,256,2,32,64]{1,0,4,3,2:T(2,128)}, s32[2,256]{1,0:T(2,128)S(1)}, /*index=5...) while((s32[]{:T(128)}, f32[2,32,64,256]{3,2,1,0:T(8,128)}, ...), condition=%wide.region_9.10_spmd, body=%wide.region_6.9_spmd.sunk | while | flops 9762522112 | bytes 51858904 | solution.py:187
  314.4 1.2 reduce-window.38
  316.7 0.6 dynamic-slice.2
  317.3 0.6 compare_convert_fusion.4
  318.3 6.3 fusion.84
  324.8 21.6 %fusion.87 = f32[1,256,2,32,64]{1,4,3,2,0:T(8,128)S(1)} fusion(f32[2,256,32,64]{1,3,2,0:T(8,128)} %fusion.84, f32[2,256,256]{2,1,0:T(8,128)S(1)} %fusion.85, f32[2,32,256]{2,1,0:T(8,128)S(1)} %copy_bitcast_fusion.4, pred[256,256]{1,0:T(8,128)(4,1)S(1)} %fusion.86, f32[2,32]{1,0:T(2,128)S(1)} %mul.647, f32[256,2,32]{0,2,1:T(8,128)S(1)} %get-tuple-element.403, ...), kind=kOutput, calls=%fused_computation.18.clone.1 | convolution fusion | flops 3245342720 | bytes 13436928 | tf_op jit(solution)/shard_map/while/body/eval_jaxpr/ghij,jghp->ighp/dot_general | solution.py:83
  346.4 6.4 copy.156
  352.8 84.6 %dynamic_update_slice.7 = f32[2,256,2,32,64]{1,0,4,3,2:T(2,128)} dynamic-update-slice(f32[2,256,2,32,64]{1,0,4,3,2:T(2,128)} %get-tuple-element.446, f32[1,256,2,32,64]{1,0,4,3,2:T(1,128)} %copy.156, s32[]{:T(128)} %get-tuple-element.443, s32[]{:T(128)} %constant.77.clone.1..sunk.1, s32[]{:T(128)} %constant.77.clone.1..sunk.1, s32[]{:T(128)} %constant.77.clone.1..sunk.1, s32[]{:T(128)} %constant.77.clone.1..sunk.1) | dynamic-update-slice | bytes 8388612 | tf_op jit(solution)/shard_map/while/body/jit(dynamic_update_index_in_dim)/dynamic_update_slice | solution.py:187
  437.3 0.6 slice.247
  437.9 0.6 exponential_multiply_fusion.2
  438.5 7.4 multiply_add_fusion.2
  446.2 1.2 reduce-window.38
  448.5 0.6 dynamic-slice.2
  449.1 0.6 compare_convert_fusion.4
  450.1 6.3 fusion.84
  456.6 21.7 %fusion.87 = f32[1,256,2,32,64]{1,4,3,2,0:T(8,128)S(1)} fusion(f32[2,256,32,64]{1,3,2,0:T(8,128)} %fusion.84, f32[2,256,256]{2,1,0:T(8,128)S(1)} %fusion.85, f32[2,32,256]{2,1,0:T(8,128)S(1)} %copy_bitcast_fusion.4, pred[256,256]{1,0:T(8,128)(4,1)S(1)} %fusion.86, f32[2,32]{1,0:T(2,128)S(1)} %mul.647, f32[256,2,32]{0,2,1:T(8,128)S(1)} %get-tuple-element.403, ...), kind=kOutput, calls=%fused_computation.18.clone.1 | convolution fusion | flops 3245342720 | bytes 13436928 | tf_op jit(solution)/shard_map/while/body/eval_jaxpr/ghij,jghp->ighp/dot_general | solution.py:83
  478.2 6.4 copy.156
  484.6 84.6 %dynamic_update_slice.7 = f32[2,256,2,32,64]{1,0,4,3,2:T(2,128)} dynamic-update-slice(f32[2,256,2,32,64]{1,0,4,3,2:T(2,128)} %get-tuple-element.446, f32[1,256,2,32,64]{1,0,4,3,2:T(1,128)} %copy.156, s32[]{:T(128)} %get-tuple-element.443, s32[]{:T(128)} %constant.77.clone.1..sunk.1, s32[]{:T(128)} %constant.77.clone.1..sunk.1, s32[]{:T(128)} %constant.77.clone.1..sunk.1, s32[]{:T(128)} %constant.77.clone.1..sunk.1) | dynamic-update-slice | bytes 8388612 | tf_op jit(solution)/shard_map/while/body/jit(dynamic_update_index_in_dim)/dynamic_update_slice | solution.py:187
  569.2 0.6 slice.247
  569.7 0.6 exponential_multiply_fusion.2
  570.3 7.4 multiply_add_fusion.2
  577.8 11.4 %multiply_reduce_fusion = f32[2,256,2]{1,0,2:T(2,128)S(1)} fusion(f32[2,256,2,32,64]{1,0,4,3,2:T(2,128)} %get-tuple-element.177, f32[2,256,2,32,64]{1,0,4,3,2:T(2,128)} %reshape.238), kind=kLoop, calls=%fused_computation.69 | loop fusion | flops 6290432 | bytes 16781312 | tf_op jit(solution)/shard_map/reduce_sum | solution.py:192
  589.2 1.0 copy.134
  590.3 1.1 copy-done
  591.4 4.2 fusion.49
  595.6 323.2 %all-gather.5.cloned.1.call-done = bf16[4096,4096]{1,0:T(8,128)(2,1)} async-done(((bf16[4096,512]{1,0:T(8,128)(2,1)}), bf16[4096,4096]{1,0:T(8,128)(2,1)}) %all-gather.5.cloned.1.call-update) | async-done | bytes 33554448 | tf_op jit(solution)/shard_map/all_gather | solution.py:201
  918.9 23.7 %convolution_convert_fusion = bf16[512,4096]{1,0:T(8,128)(2,1)} fusion(bf16[512,4096]{0,1:T(8,128)(2,1)} %fusion.49, bf16[4096,4096]{1,0:T(8,128)(2,1)} %all-gather.5.cloned.1.call-done), kind=kOutput, calls=%fused_computation.73 | convolution fusion | flops 17181966336 | bytes 41943040 | tf_op jit(solution)/shard_map/dot_general | solution.py:199
  942.5 44.7 %reduce-scatter.2.cloned.1.call-done = bf16[512,1024]{1,0:T(8,128)(2,1)} async-done(((bf16[512,4096]{1,0:T(8,128)(2,1)}), bf16[512,1024]{1,0:T(8,128)(2,1)}) %reduce-scatter.2.cloned.1.call-update) | async-done | bytes 1048592 | tf_op jit(solution)/shard_map/reduce_scatter | solution.py:204
  (93 shorter events, 4.9 us)
Async XLA Ops:
  6.5 272.9 %all-gather.7.cloned.1.call-start = ((), (), s32[]{:S(2)}) async-start(), calls=%async_computation.3 | async-start | bytes 18874368 | tf_op jit(solution)/shard_map/all_gather | solution.py:26
  8.2 20.9 %collective-permute-start = (bf16[3,5120]{1,0:T(4,128)(2,1)S(1)}, bf16[3,5120]{1,0:T(4,128)(2,1)S(1)}, u32[]{:S(2)}, u32[]{:S(2)}) collective-permute-start(bf16[3,5120]{1,0:T(4,128)(2,1)S(1)} %pad_maximum_fusion.2), channel_id=1, source_target_pairs={{0,4},{4,8},{8,12},{12,16},{16,20},{20,24},{24,28},{1,5},{5,9},{9,... | collective-permute-start | bytes 92168 | tf_op jit(solution)/shard_map/ppermute | solution.py:20
  21.9 6.6 copy-start.2
  21.9 7.1 copy-start.4
  21.9 7.1 copy-start.6
  45.0 2.8 copy-start.1
  53.5 865.3 %all-gather.5.cloned.1.call-start = ((), (), s32[]{:S(2)}) async-start(), calls=%async_computation.1 | async-start | bytes 37748736 | tf_op jit(solution)/shard_map/all_gather | solution.py:201
  54.3 933.0 %reduce-scatter.2.cloned.1.call-start = ((), (), s32[]{:S(2)}) async-start(), calls=%async_computation.2 | async-start | bytes 5242880 | tf_op jit(solution)/shard_map/reduce_scatter | solution.py:204
  84.5 10.6 %copy-start.5 = (bf16[4096]{0:T(1024)(128)(2,1)S(1)}, bf16[4096]{0:T(1024)(128)(2,1)}, u32[]{:S(2)}) copy-start(bf16[4096]{0:T(1024)(128)(2,1)} %param.29) | copy-start | bytes 24580
  281.9 32.3 %copy-start.7 = (f32[64]{0:T(128)S(1)}, f32[64]{0:T(128)}, u32[]{:S(2)}) copy-start(f32[64]{0:T(128)} %param.28) | copy-start | bytes 772
  577.8 11.4 %slice-start = ((s8[8388608]{0:T(1024)(128)(4,1)}), s8[4194304]{0:T(1024)(128)(4,1)S(1)}, s32[]{:S(2)}) async-start(s8[8388608]{0:T(1024)(128)(4,1)} %bitcast.182), calls=%async_computation.4 | async-start | bytes 8388608
  577.8 11.4 %slice-start.1 = ((s8[8388608]{0:T(1024)(128)(4,1)}), s8[4194304]{0:T(1024)(128)(4,1)S(1)}, s32[]{:S(2)}) async-start(s8[8388608]{0:T(1024)(128)(4,1)} %bitcast.182), calls=%async_computation.5 | async-start | bytes 8388608
  589.2 2.2 copy-start
  589.2 2.2 copy-start.3
Sparse Core Ops, SparseCore 0:
  53.7 225.7 all-gather.6
  281.0 637.8 all-gather.4
  942.6 44.5 reduce-scatter.1
where the time goes:
time: 1010 us; the launch traced here: 994 us
  waiting for transfers between devices  540 us (53%)
  local copies, waits for them, and re-layouts  231 us (23%)
  matrix products  101 us (10%)
  other arithmetic  87.3 us (9%)
  blocking collectives  16.2 us (2%)
  between operations  14.1 us (1%)
    all_gather x1, waiting for transfers between devices, per_device(): lax.all_gather(out_weight, 'seq', axis=1, tiled=True)  323 us
    dynamic_update_slice x4, local copies, waits for them, and re-layouts, per_device(): _, outputs = lax.scan(stepper, (state_in, seg_before), sequence)  182 us
    all_gather x1, waiting for transfers between devices, prefix(): lax.all_gather(a.astype(kind), axis)  171 us
    reduce_scatter x1, waiting for transfers between devices, per_device(): lax.psum_scatter(partial_out.astype(jnp.bfloat16), 'head', scatter_dimens...  44.7 us
    dot_general x2, matrix products, block_step(): jnp.einsum('ghij,jghp->ighp', decays * scores[:, None], scaled, precision...  43.3 us
    add x6, other arithmetic, join_states(): later[0][..., None, None] * earlier[1] + later[1]  32.3 us
    dot_general x1, matrix products, per_device(): jnp.dot(normed, lax.all_gather(out_weight, 'seq', axis=1, tiled=True), pr...  23.7 us
  transfers between devices with their start and end apart: 4, of which 3 were waited for; matrix products, arithmetic and copies ran while one was open for 37% of the time, Pallas kernels for 0%

commit v1 on v0

v1 whole, which is shorter than its diff:
```python
from functools import partial

import jax
import jax.numpy as jnp
from jax import lax
from jax.experimental import pallas as pl
from jax.experimental.pallas import tpu as pltpu
from jax.sharding import PartitionSpec as P

HEAD_DIM = 64
STATE_DIM = 256
HALO = 16
TILE = 256
STEP_HEADS = 8
LOG2E = 1.4426950408889634
SEGMENT_DROP = 200.0
EPSILON = 1e-05
BF16 = jnp.bfloat16
F32 = jnp.float32


def segment_of(positions, sequence_lengths):
    starts = jnp.cumsum(sequence_lengths) - sequence_lengths
    hits = (positions[:, None] >= starts[None, :]).astype(jnp.int32)
    return jnp.sum(hits, axis=1) - 1


def silu(v):
    return v * (0.5 * jnp.tanh(0.5 * v) + 0.5)


def conv(values, halo, masks, taps, bias):
    now = values.astype(F32)
    extended = jnp.concatenate([halo.astype(F32), now], axis=0)
    total = bias + taps[3:4] * now
    for back in range(1, 4):
        shifted = pltpu.roll(extended, back, 0)[HALO:]
        total = total + taps[3 - back : 4 - back] * (shifted * masks[:, back - 1 : back])
    return silu(total).astype(BF16)


def spread_matrix(rows, width, first_head, heads):
    row = lax.broadcasted_iota(jnp.int32, (rows, width), 0)
    col = lax.broadcasted_iota(jnp.int32, (rows, width), 1)
    return (row % heads == first_head + col // HEAD_DIM).astype(F32).astype(BF16)


def local_kernel(
    per_group_steps,
    x_ref,
    xh_ref,
    xt_ref,
    xb_ref,
    s_ref,
    sh_ref,
    st_ref,
    sb_ref,
    mask_ref,
    col_ref,
    row_ref,
    close_ref,
    skip_ref,
    y_ref,
    end_ref,
    read_ref,
    score_ref,
    write_ref,
):
    tokens = x_ref.shape[0]

    @pl.when(pl.program_id(0) % per_group_steps == 0)
    def _():
        masks = mask_ref[...]
        for part in range(2 * STATE_DIM // 128):
            lanes = slice(part * 128, part * 128 + 128)
            vec = conv(
                s_ref[:, lanes], sh_ref[:, lanes], masks, st_ref[:, lanes], sb_ref[:, lanes]
            )
            if part * 128 < STATE_DIM:
                write_ref[:, lanes] = vec
            else:
                read_ref[:, part * 128 - STATE_DIM : part * 128 - STATE_DIM + 128] = vec
        for at in range(0, tokens, TILE):
            score = lax.dot_general(
                read_ref[at : at + TILE, :],
                write_ref[: at + TILE, :],
                (((1,), (1,)), ((), ())),
                preferred_element_type=F32,
            )
            row = lax.broadcasted_iota(jnp.int32, score.shape, 0) + at
            col = lax.broadcasted_iota(jnp.int32, score.shape, 1)
            score_ref[at : at + TILE, : at + TILE] = jnp.where(row >= col, score, 0.0)

    masks = mask_ref[...]
    close = close_ref[0]
    for pair in range(STEP_HEADS // 2):
        lanes = slice(pair * 128, pair * 128 + 128)
        u = conv(x_ref[:, lanes], xh_ref[:, lanes], masks, xt_ref[:, lanes], xb_ref[:, lanes])
        weight = jnp.dot(
            close,
            spread_matrix(2 * STEP_HEADS, 128, 2 * pair, STEP_HEADS),
            preferred_element_type=F32,
        )
        weighted = (u.astype(F32) * weight).astype(BF16)
        end_ref[lanes, :] = lax.dot_general(
            weighted, write_ref[...], (((0,), (0,)), ((), ())), preferred_element_type=F32
        ).astype(BF16)
        for at in range(0, tokens, TILE):
            rows = slice(at, at + TILE)
            pieces = []
            for head in (2 * pair, 2 * pair + 1):
                here = col_ref[0, rows, head : head + 1]
                total = jnp.zeros((TILE, 128), F32)
                for back in range(0, at + TILE, TILE):
                    cols = slice(back, back + TILE)
                    gap = jnp.minimum(here - row_ref[head : head + 1, cols], 100.0)
                    mixed = (score_ref[rows, cols] * jnp.exp2(gap)).astype(BF16)
                    total = total + jnp.dot(mixed, u[cols], preferred_element_type=F32)
                pieces.append(total)
            lane = lax.broadcasted_iota(jnp.int32, (TILE, 128), 1)
            y = jnp.where(lane < HEAD_DIM, pieces[0], pieces[1])
            y_ref[rows, lanes] = (y + skip_ref[:, lanes] * u[rows].astype(F32)).astype(BF16)


def norm_kernel(y_ref, gate_ref, state_ref, read_ref, enter_ref, gain_ref, out_ref, held_ref):
    rows, width = y_ref.shape
    heads = width // HEAD_DIM
    enter = enter_ref[0]
    square = jnp.zeros((rows, 256), F32)
    for at in range(0, width, 256):
        lanes = slice(at, at + 256)
        carried = lax.dot_general(
            read_ref[...], state_ref[lanes, :], (((1,), (1,)), ((), ())), preferred_element_type=F32
        )
        factor = jnp.dot(
            enter, spread_matrix(2 * heads, 256, at // HEAD_DIM, heads), preferred_element_type=F32
        )
        y = y_ref[:, lanes].astype(F32) + carried * factor
        gated = y * silu(gate_ref[:, lanes].astype(F32))
        square = square + gated * gated
        held_ref[:, lanes] = gated
    mean = jnp.sum(square, axis=1, keepdims=True) * (1.0 / width)
    scale = lax.rsqrt(mean + EPSILON)
    for at in range(0, width, 256):
        lanes = slice(at, at + 256)
        out_ref[:, lanes] = (held_ref[:, lanes] * scale * gain_ref[:, lanes]).astype(BF16)


def split_high_low(values):
    high = lax.reduce_precision(values, 8, 7)
    return jnp.concatenate([high, values - high], axis=-1).astype(BF16)


def per_device(
    inner_input,
    state_input,
    gate_input,
    inner_taps,
    inner_bias,
    state_taps,
    state_bias,
    step_raw,
    step_bias,
    decay_log,
    skip_gain,
    norm_gain,
    out_weight,
    sequence_lengths,
):
    tokens, inner_width = inner_input.shape
    heads = step_raw.shape[0]
    groups = state_input.shape[1] // (2 * STATE_DIM)
    per_group = heads // groups
    group_width = per_group * HEAD_DIM
    seq_count = lax.axis_size("seq")
    head_count = lax.axis_size("head")
    rows_count = seq_count // 2
    seq_at = lax.axis_index("seq")
    head_at = lax.axis_index("head")
    row_at, side = seq_at // 2, seq_at % 2

    def swapped(value):
        return lax.ppermute(value, "seq", [(s, s ^ 1) for s in range(seq_count)])

    def moved(value, by):
        pairs = [(s, s + by) for s in range(seq_count) if 0 <= s + by < seq_count]
        return lax.ppermute(value, "seq", pairs)

    up, down = [out_weight], [out_weight]
    for _ in range(rows_count - 1):
        up.append(moved(up[-1], 2))
        down.append(moved(down[-1], -2))

    halo = moved(
        jnp.concatenate([inner_input[tokens - HALO :], state_input[tokens - HALO :]], axis=1), 1
    )
    positions = seq_at * tokens + lax.iota(jnp.int32, tokens + 3) - 3
    seg_extended = segment_of(positions, sequence_lengths)
    seg = seg_extended[3:]
    masks = jnp.stack(
        [(seg_extended[3 - k : 3 - k + tokens] == seg) for k in (1, 2, 3)] + [seg < 0] * 5, axis=1
    ).astype(F32)
    steps = jax.nn.softplus(step_raw + step_bias[:, None])
    running = jnp.cumsum(-jnp.exp(decay_log)[:, None] * steps, axis=1)
    running = running - SEGMENT_DROP * (seg - seg_extended[2]).astype(F32)[None, :]
    last = running[:, tokens - 1 :]
    closing = jnp.exp(last - running) * steps
    entering = jnp.exp(running)
    factor = jnp.exp(last[:, 0])
    shape = (heads // STEP_HEADS, STEP_HEADS, tokens)
    col_log = jnp.transpose((running * LOG2E).reshape(shape), (0, 2, 1))
    row_log = (running - jnp.log(steps)) * LOG2E
    close = split_high_low(jnp.transpose(closing.reshape(shape), (0, 2, 1)))
    enter = split_high_low(
        jnp.transpose(entering.reshape(groups, per_group, tokens), (0, 2, 1))
    )

    width = STEP_HEADS * HEAD_DIM
    per_steps = per_group // STEP_HEADS
    pair_width = 2 * STATE_DIM
    step_cols = lambda i: (0, i)
    group_cols = lambda i: (0, i // per_steps)
    y_local, end_state, read_all = pl.pallas_call(
        partial(local_kernel, per_steps),
        grid=(heads // STEP_HEADS,),
        in_specs=[
            pl.BlockSpec((tokens, width), step_cols),
            pl.BlockSpec((HALO, width), step_cols),
            pl.BlockSpec((4, width), step_cols),
            pl.BlockSpec((1, width), step_cols),
            pl.BlockSpec((tokens, pair_width), group_cols),
            pl.BlockSpec((HALO, pair_width), group_cols),
            pl.BlockSpec((4, pair_width), group_cols),
            pl.BlockSpec((1, pair_width), group_cols),
            pl.BlockSpec((tokens, 8), lambda i: (0, 0)),
            pl.BlockSpec((1, tokens, STEP_HEADS), lambda i: (i, 0, 0)),
            pl.BlockSpec((STEP_HEADS, tokens), lambda i: (i, 0)),
            pl.BlockSpec((1, tokens, 2 * STEP_HEADS), lambda i: (i, 0, 0)),
            pl.BlockSpec((1, width), step_cols),
        ],
        out_specs=[
            pl.BlockSpec((tokens, width), step_cols),
            pl.BlockSpec((width, STATE_DIM), lambda i: (i, 0)),
            pl.BlockSpec((tokens, STATE_DIM), group_cols),
        ],
        out_shape=[
            jax.ShapeDtypeStruct((tokens, inner_width), BF16),
            jax.ShapeDtypeStruct((inner_width, STATE_DIM), BF16),
            jax.ShapeDtypeStruct((tokens, groups * STATE_DIM), BF16),
        ],
        scratch_shapes=[
            pltpu.VMEM((tokens, tokens), F32),
            pltpu.VMEM((tokens, STATE_DIM), BF16),
        ],
        compiler_params=pltpu.CompilerParams(vmem_limit_bytes=32 * 2**20),
        cost_estimate=pl.CostEstimate(
            flops=20 * 10**9, bytes_accessed=16 * 2**20, transcendentals=12 * 10**6
        ),
        name="local_scan",
    )(
        inner_input,
        halo[:, :inner_width],
        inner_taps.astype(F32),
        inner_bias.astype(F32)[None],
        state_input,
        halo[:, inner_width:],
        state_taps.astype(F32),
        state_bias.astype(F32)[None],
        masks,
        col_log,
        row_log,
        close,
        jnp.repeat(skip_gain, HEAD_DIM)[None],
    )

    half = heads // 2
    half_rows = half * HEAD_DIM

    def half_of(value, which):
        return lax.dynamic_slice_in_dim(value, which * (value.shape[0] // 2), value.shape[0] // 2)

    def per_row(value):
        return jnp.repeat(value, HEAD_DIM)[:, None]

    factor_other = swapped(factor)
    mine, other = half_of(end_state, side), half_of(end_state, 1 - side)
    peer_end = swapped(other).astype(F32)
    mine = mine.astype(F32)
    first_end = jnp.where(side == 0, mine, peer_end)
    second_end = jnp.where(side == 0, peer_end, mine)
    first_factor = per_row(half_of(jnp.where(side == 0, factor, factor_other), side))
    second_factor = per_row(half_of(jnp.where(side == 0, factor_other, factor), side))
    pair_total = second_factor * first_end + second_end
    pair_factor = first_factor * second_factor
    window = pair_total
    for hop in range(max(1, seq_count // 4)):
        arriving = moved(window.astype(BF16), 2).astype(F32)
        window = pair_total + pair_factor * arriving
    after_first = (first_factor * arriving + first_end).astype(BF16)
    arriving = arriving.astype(BF16)
    own_part = jnp.where(side == 0, arriving, after_first)
    peer_part = swapped(jnp.where(side == 0, after_first, arriving))
    state_low = jnp.where(side == 0, own_part, peer_part)
    state_high = jnp.where(side == 0, peer_part, own_part)
    state_in = jnp.concatenate([state_low, state_high], axis=0)

    gains = norm_gain.astype(F32)[None]
    own, peer = [], []
    for group in range(groups):
        normed = pl.pallas_call(
            norm_kernel,
            grid=(tokens // TILE,),
            in_specs=[
                pl.BlockSpec((TILE, group_width), lambda i, g=group: (i, g)),
                pl.BlockSpec((TILE, group_width), lambda i, g=group: (i, g)),
                pl.BlockSpec((group_width, STATE_DIM), lambda i, g=group: (g, 0)),
                pl.BlockSpec((TILE, STATE_DIM), lambda i, g=group: (i, g)),
                pl.BlockSpec((1, TILE, 2 * per_group), lambda i, g=group: (g, i, 0)),
                pl.BlockSpec((1, group_width), lambda i, g=group: (0, g)),
            ],
            out_specs=pl.BlockSpec((TILE, group_width), lambda i: (i, 0)),
            out_shape=jax.ShapeDtypeStruct((tokens, group_width), BF16),
            scratch_shapes=[pltpu.VMEM((TILE, group_width), F32)],
            compiler_params=pltpu.CompilerParams(vmem_limit_bytes=32 * 2**20),
            cost_estimate=pl.CostEstimate(
                flops=10**9, bytes_accessed=8 * 2**20, transcendentals=10**6
            ),
            name="gated_norm",
        )(y_local, gate_input, state_in, read_all, enter, gains)
        own.append(normed)
        peer.append(swapped(normed))
    own = jnp.concatenate(own, axis=1)
    peer = jnp.concatenate(peer, axis=1)
    acts = jnp.concatenate([own, peer], axis=0)

    partials = []
    for distance in range(rows_count):
        if distance == 0:
            weight = out_weight
        else:
            weight = jnp.where(row_at >= distance, up[distance], down[rows_count - distance])
        partials.append(jnp.dot(acts, weight, preferred_element_type=F32).astype(BF16))
    stacked = jnp.stack(partials)
    ordered = [
        lax.dynamic_index_in_dim(stacked, (row_at - at) % rows_count, 0, False)
        for at in range(rows_count)
    ]
    per_head = rows_count // head_count
    blocks = jnp.stack(ordered).reshape(head_count, per_head, *partials[0].shape)
    bit = 1
    while bit < head_count:
        high = blocks.shape[0] // 2
        split = blocks.reshape(high, 2, *blocks.shape[1:])
        mine_bit = (head_at // bit) % 2
        keep = lax.dynamic_index_in_dim(split, mine_bit, 1, False)
        send = lax.dynamic_index_in_dim(split, 1 - mine_bit, 1, False)
        got = lax.ppermute(send, "head", [(h, h ^ bit) for h in range(head_count)])
        blocks = (keep.astype(F32) + got.astype(F32)).astype(BF16)
        bit *= 2
    final = blocks[0]
    mine_out = final[:, :tokens]
    peer_out = swapped(final[:, tokens:])
    even = jnp.where(side == 0, mine_out, peer_out)
    odd = jnp.where(side == 0, peer_out, mine_out)
    both = jnp.stack([even, odd], axis=1)
    return jnp.transpose(both, (2, 0, 1, 3)).reshape(tokens, -1)


def solution(mesh):
    in_specs = (
        P("seq", "head"),
        P("seq", "head"),
        P("seq", "head"),
        P(None, "head"),
        P("head"),
        P(None, "head"),
        P("head"),
        P("head", "seq"),
        P("head"),
        P("head"),
        P("head"),
        P("head"),
        P("head", "seq"),
        P(),
    )
    out_specs = P("seq", "head")
    return jax.shard_map(
        per_device, mesh=mesh, in_specs=in_specs, out_specs=out_specs, check_vma=False
    )
```

time: 1010 us -> 467 us (0.46)
  waiting for transfers between devices: 540 us -> 277 us
  local copies, waits for them, and re-layouts: 231 us -> 19.9 us
  other arithmetic: 87.3 us -> 28 us
  matrix products: 101 us -> 67.9 us
  starting transfers between devices: 3.48 us -> 35 us
  Pallas kernels: 0 us -> 31.1 us
  blocking collectives: 16.2 us -> 0 us
  between operations: 14.1 us -> 1.06 us
    all_gather x2 -> x0, waiting for transfers between devices: 494 us -> none  [the longest x1 323 us: per_device(): lax.all_gather(out_weight, 'seq', axis=1, tiled=True)]
    ppermute x1 -> x17, waiting for transfers between devices: 0.01 us -> 277 us  [the longest x9 168 us: moved(): return lax.ppermute(value, 'seq', pairs)]
    dynamic_update_slice x4 -> x0, local copies, waits for them, and re-layouts: 182 us -> none  [per_device(): _, outputs = lax.scan(stepper, (state_in, seg_before), sequence)]
    reduce_scatter x1 -> x0, waiting for transfers between devices: 44.7 us -> none  [per_device(): lax.psum_scatter(partial_out.astype(jnp.bfloat16), 'head', scatter_dimens...]
    dot_general x10 -> x4, matrix products: 101 us -> 67.9 us  [per_device(): jnp.dot(acts, weight, preferred_element_type=F32).astype(BF16)]
    add x6 -> x0, other arithmetic: 32.3 us -> none  [join_states(): later[0][..., None, None] * earlier[1] + later[1]]
    ppermute x1 -> x17, starting transfers between devices: 3.4 us -> 35 us  [the longest x9 27.2 us: moved(): return lax.ppermute(value, 'seq', pairs)]
    pallas_call x0 -> x3, Pallas kernels: none -> 31.1 us  [the longest x1 24.5 us: per_device(): pl.pallas_call(partial(local_kernel, per_steps), grid=(heads // STEP_HEAD...]
  transfers between devices with their start and end apart: 4 -> 17, of which waited for: 3 -> 12; matrix products, arithmetic and copies ran while one was open for 37% -> 17% of each run, Pallas kernels for 0% -> 7%
where the time goes in v1:
time: 467 us; the launch traced here: 460 us
  waiting for transfers between devices  277 us (59%)
  matrix products  67.9 us (15%)
  starting transfers between devices  35 us (7%)
  Pallas kernels  31.1 us (7%)
  other arithmetic  28 us (6%)
  local copies, waits for them, and re-layouts  19.9 us (4%)
    ppermute x9, waiting for transfers between devices, moved(): return lax.ppermute(value, 'seq', pairs)  168 us
    ppermute x6, waiting for transfers between devices, swapped(): return lax.ppermute(value, 'seq', [(s, s ^ 1) for s in range(seq_count)])  80.7 us
    dot_general x4, matrix products, per_device(): jnp.dot(acts, weight, preferred_element_type=F32).astype(BF16)  67.9 us
    ppermute x2, waiting for transfers between devices, per_device(): got = lax.ppermute(send, 'head', [(h, h ^ bit) for h in range(head_count)])  28 us
    ppermute x9, starting transfers between devices, moved(): return lax.ppermute(value, 'seq', pairs)  27.2 us
    pallas_call x1, Pallas kernels, per_device(): pl.pallas_call(partial(local_kernel, per_steps), grid=(heads // STEP_HEAD...  24.5 us
    unnamed x30, local copies, waits for them, and re-layouts  11.1 us
  transfers between devices with their start and end apart: 17, of which 12 were waited for; matrix products, arithmetic and copies ran while one was open for 17% of the time, Pallas kernels for 7%

profile of v1, /device:TPU:24, one launch (start us, length us, event | category | flops | bytes accessed | tf_op | source)
XLA Modules:
  0.0 459.6 jit_solution(17164280322964490380)
XLA Ops:
  0.0 0.9 slice.42
  0.9 0.8 slice.43
  1.7 3.4 collective-permute-start
  5.1 4.3 collective-permute-start.9
  9.4 0.8 reduce-window.19
  10.2 0.7 bitcast_subtract_fusion.1
  11.0 0.6 slice.52
  11.6 0.7 convert_multiply_fusion
  12.3 0.7 exponential_negate_fusion
  12.9 1.1 copy_bitcast_fusion
  14.0 1.2 reduce-window.20
  15.6 1.1 subtract_multiply_fusion
  16.8 1.1 reduce-precision_convert_fusion.1
  18.0 1.3 copy.58.close_ref
  19.5 0.6 copy.54
  20.1 1.6 multiply_bitcast_fusion.col_ref
  22.3 1.6 copy-done.3
  23.9 1.2 copy-done.4
  25.2 2.2 copy-done.5
  27.3 1.2 copy-done.6
  28.6 24.5 %local_scan.1 = (bf16[512,4096]{1,0:T(8,128)(2,1)S(1)}, bf16[4096,256]{1,0:T(8,128)(2,1)S(1)}, bf16[512,512]{1,0:T(8,128)(2,1)S(1)}) custom-call(bf16[512,4096]{1,0:T(8,128)(2,1)S(1)} %copy-done.5, bf16[16,4096]{1,0:T(8,128)(2,1)S(1)} %slice.56.xh_ref, f32[4,4096]{1,0:T(4,128)S(1)} %convert_element_type.85.xt_ref, f32[1,4096]{1,0:T(1,128)S(1)} %bitcast.54, ...), custom_call_target="tpu_custom_call" | custom-call | flops 20000000000 | bytes 16777216 | tf_op jit(solution)/shard_map/local_scan/pallas_call | solution.py:223
  53.0 1.9 copy-done.1
  55.0 1.0 constant_dynamic-slice_fusion.5
  56.0 1.5 collective-permute-start.2
  57.5 1.3 collective-permute-start.8
  58.8 0.5 collective-permute-start.1
  59.4 21.3 %collective-permute-done.1 = f32[64]{0:T(128)S(1)} collective-permute-done((f32[64]{0:T(128)S(1)}, f32[64]{0:T(128)S(1)}, u32[]{:S(2)}, u32[]{:S(2)}) %collective-permute-start.1) | collective-permute-done | bytes 288 | tf_op jit(solution)/shard_map/ppermute | solution.py:183
  80.9 2.7 fusion.11
  83.6 1.3 collective-permute-start.3
  85.1 88.6 %collective-permute-done.3 = bf16[2048,256]{1,0:T(8,128)(2,1)} collective-permute-done((bf16[2048,256]{1,0:T(8,128)(2,1)}, bf16[2048,256]{1,0:T(8,128)(2,1)}, u32[]{:S(2)}, u32[]{:S(2)}) %collective-permute-start.3) | collective-permute-done | bytes 1048608 | tf_op jit(solution)/shard_map/ppermute | solution.py:187
  173.7 2.1 add_convert_fusion.2
  175.8 1.3 collective-permute-start.4
  177.1 6.5 %collective-permute-start.10 = (bf16[4096,512]{1,0:T(8,128)(2,1)}, bf16[4096,512]{1,0:T(8,128)(2,1)}, u32[]{:S(2)}, u32[]{:S(2)}) collective-permute-start(bf16[4096,512]{1,0:T(8,128)(2,1)} %collective-permute-done.9), channel_id=1, source_target_pairs={{8,0},{12,4},{16,8},{20,12},{24,16},{28,20},{9,1},{13,5},{17,9},{2... | collective-permute-start | bytes 12582920 | tf_op jit(solution)/shard_map/ppermute | solution.py:187
  183.6 17.2 %collective-permute-done.4 = bf16[2048,256]{1,0:T(8,128)(2,1)S(1)} collective-permute-done((bf16[2048,256]{1,0:T(8,128)(2,1)S(1)}, bf16[2048,256]{1,0:T(8,128)(2,1)S(1)}, u32[]{:S(2)}, u32[]{:S(2)}) %collective-permute-start.4) | collective-permute-done | bytes 1048608 | tf_op jit(solution)/shard_map/ppermute | solution.py:187
  200.8 1.0 copy-done.8
  201.8 2.8 broadcast_select_fusion.2
  205.0 1.5 collective-permute-start.12
  207.1 19.9 %collective-permute-done.5 = bf16[2048,256]{1,0:T(8,128)(2,1)} collective-permute-done((bf16[2048,256]{1,0:T(8,128)(2,1)}, bf16[2048,256]{1,0:T(8,128)(2,1)}, u32[]{:S(2)}, u32[]{:S(2)}) %collective-permute-start.5) | collective-permute-done | bytes 1048608 | tf_op jit(solution)/shard_map/ppermute | solution.py:183
  227.1 3.0 broadcast_select_fusion.1
  230.3 2.8 gated_norm.2
  233.1 3.8 gated_norm.3
  237.4 1.5 collective-permute-start.7
  239.0 30.8 %collective-permute-done.10 = bf16[4096,512]{1,0:T(8,128)(2,1)} collective-permute-done((bf16[4096,512]{1,0:T(8,128)(2,1)}, bf16[4096,512]{1,0:T(8,128)(2,1)}, u32[]{:S(2)}, u32[]{:S(2)}) %collective-permute-start.10) | collective-permute-done | bytes 4194336 | tf_op jit(solution)/shard_map/ppermute | solution.py:187
  269.7 6.4 %collective-permute-start.11 = (bf16[4096,512]{1,0:T(8,128)(2,1)}, bf16[4096,512]{1,0:T(8,128)(2,1)}, u32[]{:S(2)}, u32[]{:S(2)}) collective-permute-start(bf16[4096,512]{1,0:T(8,128)(2,1)} %collective-permute-done.10), channel_id=1, source_target_pairs={{8,0},{12,4},{16,8},{20,12},{24,16},{28,20},{9,1},{13,5},{17,9},{2... | collective-permute-start | bytes 12582920 | tf_op jit(solution)/shard_map/ppermute | solution.py:187
  276.1 20.5 %collective-permute-done.12 = bf16[4096,512]{1,0:T(8,128)(2,1)} collective-permute-done((bf16[4096,512]{1,0:T(8,128)(2,1)}, bf16[4096,512]{1,0:T(8,128)(2,1)}, u32[]{:S(2)}, u32[]{:S(2)}) %collective-permute-start.12) | collective-permute-done | bytes 4194336 | tf_op jit(solution)/shard_map/ppermute | solution.py:187
  296.6 1.3 collective-permute-start.13
  297.9 27.9 %collective-permute-done.7 = bf16[512,2048]{1,0:T(8,128)(2,1)} collective-permute-done((bf16[512,2048]{1,0:T(8,128)(2,1)}, bf16[512,2048]{1,0:T(8,128)(2,1)}, u32[]{:S(2)}, u32[]{:S(2)}) %collective-permute-start.7) | collective-permute-done | bytes 2097184 | tf_op jit(solution)/shard_map/ppermute | solution.py:183
  325.7 16.0 %fusion.30 = bf16[1,1024,512]{1,2,0:T(8,128)(2,1)S(1)} fusion(bf16[4096,512]{1,0:T(8,128)(2,1)} %param.26, bf16[512,2048]{1,0:T(8,128)(2,1)} %collective-permute-done.7, bf16[512,2048]{1,0:T(8,128)(2,1)} %collective-permute-done.6, bf16[512,2048]{1,0:T(8,128)(2,1)} %gated_norm.3, bf16[512,2048]{1,0:T(8,128)(2,1)S(1)} %gated_norm.2), kind=kOutput, calls=%fused_computation.31 | convolution fusion | flops 4329046016 | bytes 13631488 | tf_op jit(solution)/shard_map/dot_general | solution.py:342
  341.8 17.4 %fusion.24 = bf16[1,1024,512]{1,2,0:T(8,128)(2,1)} fusion(bf16[4096,512]{1,0:T(8,128)(2,1)} %collective-permute-done.12, bf16[4096,512]{1,0:T(8,128)(2,1)} %collective-permute-done.10, pred[]{:T(512)S(6)} %ge.26, bf16[512,2048]{1,0:T(8,128)(2,1)} %collective-permute-done.7, bf16[512,2048]{1,0:T(8,128)(2,1)} %collective-permute-done.6, ...), kind=kOutput, calls=%fused_computation.29 | convolution fusion | flops 4331143168 | bytes 17825792 | tf_op jit(solution)/shard_map/dot_general | solution.py:342
  359.1 2.1 collective-permute-done.11
  361.3 17.1 %fusion.27 = bf16[1,1024,512]{1,2,0:T(8,128)(2,1)} fusion(bf16[4096,512]{1,0:T(8,128)(2,1)} %collective-permute-done.8, bf16[4096,512]{1,0:T(8,128)(2,1)} %collective-permute-done.11, pred[]{:T(512)S(6)} %ge.25, bf16[512,2048]{1,0:T(8,128)(2,1)} %collective-permute-done.7, bf16[512,2048]{1,0:T(8,128)(2,1)} %collective-permute-done.6, ...), kind=kOutput, calls=%fused_computation.30 | convolution fusion | flops 4331143168 | bytes 17825792 | tf_op jit(solution)/shard_map/dot_general | solution.py:342
  378.4 8.8 %collective-permute-done.13 = bf16[4096,512]{1,0:T(8,128)(2,1)} collective-permute-done((bf16[4096,512]{1,0:T(8,128)(2,1)}, bf16[4096,512]{1,0:T(8,128)(2,1)}, u32[]{:S(2)}, u32[]{:S(2)}) %collective-permute-start.13) | collective-permute-done | bytes 4194336 | tf_op jit(solution)/shard_map/ppermute | solution.py:187
  387.2 17.4 %fusion.21 = bf16[1,1024,512]{1,2,0:T(8,128)(2,1)} fusion(bf16[4096,512]{1,0:T(8,128)(2,1)} %collective-permute-done.13, bf16[4096,512]{1,0:T(8,128)(2,1)} %collective-permute-done.9, pred[]{:T(512)S(6)} %ge.27, bf16[512,2048]{1,0:T(8,128)(2,1)} %collective-permute-done.7, bf16[512,2048]{1,0:T(8,128)(2,1)} %collective-permute-done.6, ...), kind=kOutput, calls=%fused_computation.28 | convolution fusion | flops 4331143168 | bytes 17825792 | tf_op jit(solution)/shard_map/dot_general | solution.py:342
  404.5 2.1 pad_maximum_fusion
  407.1 0.6 pad_maximum_fusion.1
  407.7 1.9 copy-done.7
  409.9 4.2 collective-permute-done.14
  414.2 3.2 fusion
  417.4 1.6 collective-permute-start.15
  419.0 23.8 %collective-permute-done.15 = bf16[1,1,1024,512]{2,3,0,1:T(8,128)(2,1)} collective-permute-done((bf16[1,1,1024,512]{2,3,0,1:T(8,128)(2,1)S(1)}, bf16[1,1,1024,512]{2,3,0,1:T(8,128)(2,1)}, u32[]{:S(2)}, u32[]{:S(2)}) %collective-permute-start.15) | collective-permute-done | bytes 1048608 | tf_op jit(solution)/shard_map/ppermute | solution.py:357
  442.8 1.6 fusion.31
  444.5 1.6 collective-permute-start.16
  446.1 11.6 %collective-permute-done.16 = bf16[1,512,512]{1,2,0:T(8,128)(2,1)S(1)} collective-permute-done((bf16[1,512,512]{1,2,0:T(8,128)(2,1)S(1)}, bf16[1,512,512]{1,2,0:T(8,128)(2,1)S(1)}, u32[]{:S(2)}, u32[]{:S(2)}) %collective-permute-start.16) | collective-permute-done | bytes 524320 | tf_op jit(solution)/shard_map/ppermute | solution.py:183
  457.9 1.3 copy.63
  (80 shorter events, 4.4 us)
Async XLA Ops:
  1.7 20.6 %collective-permute-start = (bf16[16,5120]{1,0:T(8,128)(2,1)S(1)}, bf16[16,5120]{1,0:T(8,128)(2,1)S(1)}, u32[]{:S(2)}, u32[]{:S(2)}) collective-permute-start(bf16[16,5120]{1,0:T(8,128)(2,1)S(1)} %pad_maximum_fusion.5), channel_id=1, source_target_pairs={{0,4},{4,8},{8,12},{12,16},{16,20},{20,24},{24,28},{1,5},{5,9},{9,... | collective-permute-start | bytes 491528 | tf_op jit(solution)/shard_map/ppermute | solution.py:187
  5.1 172.0 %collective-permute-start.9 = (bf16[4096,512]{1,0:T(8,128)(2,1)}, bf16[4096,512]{1,0:T(8,128)(2,1)}, u32[]{:S(2)}, u32[]{:S(2)}) collective-permute-start(bf16[4096,512]{1,0:T(8,128)(2,1)} %param.26), channel_id=1, source_target_pairs={{8,0},{12,4},{16,8},{20,12},{24,16},{28,20},{9,1},{13,5},{17,9},{2... | collective-permute-start | bytes 12582920 | tf_op jit(solution)/shard_map/ppermute | solution.py:187
  17.9 4.1 copy-start.9
  18.0 4.1 copy-start.14
  18.0 4.3 copy-start.10
  18.0 4.3 copy-start.11
  18.0 4.3 copy-start.13
  22.3 1.6 copy-start.3
  23.9 1.2 copy-start.4
  25.2 2.2 copy-start.5
  27.3 1.2 copy-start.6
  53.0 1.9 copy-start.1
  56.0 24.9 %collective-permute-start.2 = (bf16[2048,256]{1,0:T(8,128)(2,1)}, bf16[2048,256]{1,0:T(8,128)(2,1)}, u32[]{:S(2)}, u32[]{:S(2)}) collective-permute-start(bf16[2048,256]{1,0:T(8,128)(2,1)} %constant_dynamic-slice_fusion.5), channel_id=1, source_target_pairs={{0,4},{4,0},{8,12},{12,8},{16,20},{20,16},{24,28},{28,24},{1,5},{5... | collective-permute-start | bytes 3145736 | tf_op jit(solution)/shard_map/ppermute | solution.py:183
  57.5 147.5 %collective-permute-start.8 = (bf16[4096,512]{1,0:T(8,128)(2,1)}, bf16[4096,512]{1,0:T(8,128)(2,1)}, u32[]{:S(2)}, u32[]{:S(2)}) collective-permute-start(bf16[4096,512]{1,0:T(8,128)(2,1)} %param.26), channel_id=1, source_target_pairs={{0,8},{4,12},{8,16},{12,20},{16,24},{20,28},{1,9},{5,13},{9,17},{1... | collective-permute-start | bytes 12582920 | tf_op jit(solution)/shard_map/ppermute | solution.py:187
  58.8 21.8 %collective-permute-start.1 = (f32[64]{0:T(128)S(1)}, f32[64]{0:T(128)S(1)}, u32[]{:S(2)}, u32[]{:S(2)}) collective-permute-start(f32[64]{0:T(128)S(1)} %exp.20), channel_id=1, source_target_pairs={{0,4},{4,0},{8,12},{12,8},{16,20},{20,16},{24,28},{28,24},{1,5},{5... | collective-permute-start | bytes 776 | tf_op jit(solution)/shard_map/ppermute | solution.py:183
  83.6 90.1 %collective-permute-start.3 = (bf16[2048,256]{1,0:T(8,128)(2,1)}, bf16[2048,256]{1,0:T(8,128)(2,1)}, u32[]{:S(2)}, u32[]{:S(2)}) collective-permute-start(bf16[2048,256]{1,0:T(8,128)(2,1)} %fusion.11), channel_id=1, source_target_pairs={{0,8},{4,12},{8,16},{12,20},{16,24},{20,28},{1,9},{5,13},{9,17},{1... | collective-permute-start | bytes 3145736 | tf_op jit(solution)/shard_map/ppermute | solution.py:187
  85.1 121.7 %copy-start.12 = (bf16[4096]{0:T(1024)(128)(2,1)S(1)}, bf16[4096]{0:T(1024)(128)(2,1)}, u32[]{:S(2)}) copy-start(bf16[4096]{0:T(1024)(128)(2,1)} %param.25) | copy-start | bytes 24580
  175.8 25.0 %collective-permute-start.4 = (bf16[2048,256]{1,0:T(8,128)(2,1)S(1)}, bf16[2048,256]{1,0:T(8,128)(2,1)S(1)}, u32[]{:S(2)}, u32[]{:S(2)}) collective-permute-start(bf16[2048,256]{1,0:T(8,128)(2,1)S(1)} %add_convert_fusion.2), channel_id=1, source_target_pairs={{0,8},{4,12},{8,16},{12,20},{16,24},{20,28},{1,9},{5,13},{9,17},{1... | collective-permute-start | bytes 3145736 | tf_op jit(solution)/shard_map/ppermute | solution.py:187
  177.1 92.6 %collective-permute-start.10 = (bf16[4096,512]{1,0:T(8,128)(2,1)}, bf16[4096,512]{1,0:T(8,128)(2,1)}, u32[]{:S(2)}, u32[]{:S(2)}) collective-permute-start(bf16[4096,512]{1,0:T(8,128)(2,1)} %collective-permute-done.9), channel_id=1, source_target_pairs={{8,0},{12,4},{16,8},{20,12},{24,16},{28,20},{9,1},{13,5},{17,9},{2... | collective-permute-start | bytes 12582920 | tf_op jit(solution)/shard_map/ppermute | solution.py:187
  200.8 1.0 copy-start.8
  204.5 22.5 %collective-permute-start.5 = (bf16[2048,256]{1,0:T(8,128)(2,1)}, bf16[2048,256]{1,0:T(8,128)(2,1)}, u32[]{:S(2)}, u32[]{:S(2)}) collective-permute-start(bf16[2048,256]{1,0:T(8,128)(2,1)} %broadcast_select_fusion.2), channel_id=1, source_target_pairs={{0,4},{4,0},{8,12},{12,8},{16,20},{20,16},{24,28},{28,24},{1,5},{5... | collective-permute-start | bytes 3145736 | tf_op jit(solution)/shard_map/ppermute | solution.py:183
  205.0 91.5 %collective-permute-start.12 = (bf16[4096,512]{1,0:T(8,128)(2,1)}, bf16[4096,512]{1,0:T(8,128)(2,1)}, u32[]{:S(2)}, u32[]{:S(2)}) collective-permute-start(bf16[4096,512]{1,0:T(8,128)(2,1)} %collective-permute-done.8), channel_id=1, source_target_pairs={{0,8},{4,12},{8,16},{12,20},{16,24},{20,28},{1,9},{5,13},{9,17},{1... | collective-permute-start | bytes 12582920 | tf_op jit(solution)/shard_map/ppermute | solution.py:187
  207.1 23.1 %copy-start = (bf16[512,4096]{1,0:T(8,128)(2,1)S(1)}, bf16[512,4096]{1,0:T(8,128)(2,1)}, u32[]{:S(2)}) copy-start(bf16[512,4096]{1,0:T(8,128)(2,1)} %gate_ref.3) | copy-start | bytes 12582916
  207.1 23.1 %copy-start.2 = (bf16[512,4096]{1,0:T(8,128)(2,1)S(1)}, bf16[512,4096]{1,0:T(8,128)(2,1)}, u32[]{:S(2)}) copy-start(bf16[512,4096]{1,0:T(8,128)(2,1)} %copy-done.1) | copy-start | bytes 12582916
  236.9 60.9 %collective-permute-start.6 = (bf16[512,2048]{1,0:T(8,128)(2,1)S(1)}, bf16[512,2048]{1,0:T(8,128)(2,1)}, u32[]{:S(2)}, u32[]{:S(2)}) collective-permute-start(bf16[512,2048]{1,0:T(8,128)(2,1)S(1)} %gated_norm.2), channel_id=1, source_target_pairs={{0,4},{4,0},{8,12},{12,8},{16,20},{20,16},{24,28},{28,24},{1,5},{5... | collective-permute-start | bytes 6291464 | tf_op jit(solution)/shard_map/ppermute | solution.py:183
  237.4 88.3 %collective-permute-start.7 = (bf16[512,2048]{1,0:T(8,128)(2,1)}, bf16[512,2048]{1,0:T(8,128)(2,1)}, u32[]{:S(2)}, u32[]{:S(2)}) collective-permute-start(bf16[512,2048]{1,0:T(8,128)(2,1)} %gated_norm.3), channel_id=1, source_target_pairs={{0,4},{4,0},{8,12},{12,8},{16,20},{20,16},{24,28},{28,24},{1,5},{5... | collective-permute-start | bytes 6291464 | tf_op jit(solution)/shard_map/ppermute | solution.py:183
  269.7 91.5 %collective-permute-start.11 = (bf16[4096,512]{1,0:T(8,128)(2,1)}, bf16[4096,512]{1,0:T(8,128)(2,1)}, u32[]{:S(2)}, u32[]{:S(2)}) collective-permute-start(bf16[4096,512]{1,0:T(8,128)(2,1)} %collective-permute-done.10), channel_id=1, source_target_pairs={{8,0},{12,4},{16,8},{20,12},{24,16},{28,20},{9,1},{13,5},{17,9},{2... | collective-permute-start | bytes 12582920 | tf_op jit(solution)/shard_map/ppermute | solution.py:187
  296.6 90.6 %collective-permute-start.13 = (bf16[4096,512]{1,0:T(8,128)(2,1)}, bf16[4096,512]{1,0:T(8,128)(2,1)}, u32[]{:S(2)}, u32[]{:S(2)}) collective-permute-start(bf16[4096,512]{1,0:T(8,128)(2,1)} %collective-permute-done.12), channel_id=1, source_target_pairs={{0,8},{4,12},{8,16},{12,20},{16,24},{20,28},{1,9},{5,13},{9,17},{1... | collective-permute-start | bytes 12582920 | tf_op jit(solution)/shard_map/ppermute | solution.py:187
  407.7 1.9 copy-start.7
  409.8 4.4 collective-permute-start.14
  417.4 25.4 %collective-permute-start.15 = (bf16[1,1,1024,512]{2,3,0,1:T(8,128)(2,1)S(1)}, bf16[1,1,1024,512]{2,3,0,1:T(8,128)(2,1)}, u32[]{:S(2)}, u32[]{:S(2)}) collective-permute-start(bf16[1,1,1024,512]{2,3,0,1:T(8,128)(2,1)S(1)} %constant_dynamic-slice_fusion), channel_id=1, source_target_pairs={{0,2},{1,3},{2,0},{3,1},{4,6},{5,7},{6,4},{7,5},{8,10},{9,11},{10,... | collective-permute-start | bytes 3145736 | tf_op jit(solution)/shard_map/ppermute | solution.py:357
  444.5 13.2 %collective-permute-start.16 = (bf16[1,512,512]{1,2,0:T(8,128)(2,1)S(1)}, bf16[1,512,512]{1,2,0:T(8,128)(2,1)S(1)}, u32[]{:S(2)}, u32[]{:S(2)}) collective-permute-start(bf16[1,512,512]{1,2,0:T(8,128)(2,1)S(1)} %slice.61), channel_id=1, source_target_pairs={{0,4},{4,0},{8,12},{12,8},{16,20},{20,16},{24,28},{28,24},{1,5},{5... | collective-permute-start | bytes 1572872 | tf_op jit(solution)/shard_map/ppermute | solution.py:183

commit v2 on v1

--- a/solution.py
+++ b/solution.py
@@ -144,6 +144,55 @@
     for at in range(0, width, 256):
         lanes = slice(at, at + 256)
         out_ref[:, lanes] = (held_ref[:, lanes] * scale * gain_ref[:, lanes]).astype(BF16)
+
+
+def project_kernel(depth, first_ref, *refs):
+    acts, (one_ref, two_ref, out_ref) = refs[:-3], refs[-3:]
+    tokens, width = acts[0].shape
+    parts = depth // width
+
+    def multiply(weight_ref):
+        for half in range(2):
+            total = jnp.zeros((tokens, weight_ref.shape[1]), F32)
+            for part in range(parts):
+                total = total + jnp.dot(
+                    acts[half * parts + part][...],
+                    weight_ref[part * width : part * width + width, :],
+                    preferred_element_type=F32,
+                )
+            out_ref[half * tokens : half * tokens + tokens, :] = total.astype(BF16)
+
+    @pl.when(first_ref[0] == 1)
+    def _():
+        multiply(one_ref)
+
+    @pl.when(first_ref[0] != 1)
+    def _():
+        multiply(two_ref)
+
+
+def project(acts, one, two, first):
+    tokens, width = acts[0].shape
+    depth, features = one.shape
+    tile = min(features, 256)
+    whole = pl.BlockSpec((tokens, width), lambda i, f: (0, 0))
+    return pl.pallas_call(
+        partial(project_kernel, depth),
+        grid_spec=pltpu.PrefetchScalarGridSpec(
+            num_scalar_prefetch=1,
+            grid=(features // tile,),
+            in_specs=[whole] * len(acts)
+            + [
+                pl.BlockSpec((depth, tile), lambda i, f: (0, i * f[0])),
+                pl.BlockSpec((depth, tile), lambda i, f: (0, i * (1 - f[0]))),
+            ],
+            out_specs=pl.BlockSpec((2 * tokens, tile), lambda i, f: (0, i)),
+        ),
+        out_shape=jax.ShapeDtypeStruct((2 * tokens, features), BF16),
+        compiler_params=pltpu.CompilerParams(vmem_limit_bytes=48 * 2**20),
+        cost_estimate=pl.CostEstimate(flops=10**6, bytes_accessed=10**6, transcendentals=0),
+        name="project",
+    )(first, *acts, one, two)
 
 
 def split_high_low(values):
@@ -254,7 +303,7 @@
         ],
         compiler_params=pltpu.CompilerParams(vmem_limit_bytes=32 * 2**20),
         cost_estimate=pl.CostEstimate(
-            flops=20 * 10**9, bytes_accessed=16 * 2**20, transcendentals=12 * 10**6
+            flops=10**6, bytes_accessed=10**6, transcendentals=0
         ),
         name="local_scan",
     )(
@@ -323,41 +372,43 @@
             scratch_shapes=[pltpu.VMEM((TILE, group_width), F32)],
             compiler_params=pltpu.CompilerParams(vmem_limit_bytes=32 * 2**20),
             cost_estimate=pl.CostEstimate(
-                flops=10**9, bytes_accessed=8 * 2**20, transcendentals=10**6
+                flops=10**6, bytes_accessed=10**6, transcendentals=0
             ),
             name="gated_norm",
         )(y_local, gate_input, state_in, read_all, enter, gains)
         own.append(normed)
         peer.append(swapped(normed))
-    own = jnp.concatenate(own, axis=1)
-    peer = jnp.concatenate(peer, axis=1)
-    acts = jnp.concatenate([own, peer], axis=0)
-
-    partials = []
+    acts = own + peer
+
+    per_head = rows_count // head_count
+    reduced = []
     for distance in range(rows_count):
         if distance == 0:
-            weight = out_weight
+            one, two, first = out_weight, out_weight, jnp.ones((1,), jnp.int32)
         else:
-            weight = jnp.where(row_at >= distance, up[distance], down[rows_count - distance])
-        partials.append(jnp.dot(acts, weight, preferred_element_type=F32).astype(BF16))
-    stacked = jnp.stack(partials)
-    ordered = [
-        lax.dynamic_index_in_dim(stacked, (row_at - at) % rows_count, 0, False)
-        for at in range(rows_count)
-    ]
-    per_head = rows_count // head_count
-    blocks = jnp.stack(ordered).reshape(head_count, per_head, *partials[0].shape)
-    bit = 1
-    while bit < head_count:
-        high = blocks.shape[0] // 2
-        split = blocks.reshape(high, 2, *blocks.shape[1:])
-        mine_bit = (head_at // bit) % 2
-        keep = lax.dynamic_index_in_dim(split, mine_bit, 1, False)
-        send = lax.dynamic_index_in_dim(split, 1 - mine_bit, 1, False)
-        got = lax.ppermute(send, "head", [(h, h ^ bit) for h in range(head_count)])
-        blocks = (keep.astype(F32) + got.astype(F32)).astype(BF16)
-        bit *= 2
-    final = blocks[0]
+            one, two = up[distance], down[rows_count - distance]
+            first = (row_at >= distance).astype(jnp.int32)[None]
+        value = project(acts, one, two, first)
+        bit = 1
+        while bit < head_count:
+            pairs = []
+            for s in range(seq_count):
+                owner = (s // 2 - distance) % rows_count // per_head
+                for h in range(head_count):
+                    if h % bit == owner % bit and (h ^ owner) & bit:
+                        pairs.append((s * head_count + h, s * head_count + (h ^ bit)))
+            got = lax.ppermute(value, ("seq", "head"), pairs)
+            value = (value.astype(F32) + got.astype(F32)).astype(BF16)
+            bit *= 2
+        reduced.append(value)
+    finals = []
+    for shard in range(per_head):
+        wanted = (row_at - head_at * per_head - shard) % rows_count
+        chosen = reduced[0]
+        for distance in range(1, rows_count):
+            chosen = jnp.where(wanted == distance, reduced[distance], chosen)
+        finals.append(chosen)
+    final = jnp.stack(finals)
     mine_out = final[:, :tokens]
     peer_out = swapped(final[:, tokens:])
     even = jnp.where(side == 0, mine_out, peer_out)

time: 467 us -> 529 us (1.13); the launches traced: 460 us -> 528 us
  waiting for transfers between devices: 277 us -> 349 us
  matrix products: 67.9 us -> 0 us
  Pallas kernels: 31.1 us -> 64.6 us
  starting transfers between devices: 35 us -> 54.4 us
  local copies, waits for them, and re-layouts: 19.9 us -> 30.8 us
    dot_general x4 -> x0, matrix products: 67.9 us -> none  [per_device(): jnp.dot(acts, weight, preferred_element_type=F32).astype(BF16)]
    ppermute x6, waiting for transfers between devices: 80.7 us -> 131 us  [swapped(): return lax.ppermute(value, 'seq', [(s, s ^ 1) for s in range(seq_count)])]
    pallas_call x0 -> x4, Pallas kernels: none -> 34.5 us  [project(): pl.pallas_call(partial(project_kernel, depth), grid_spec=pltpu.PrefetchSc...]
    ppermute x9, waiting for transfers between devices: 168 us -> 200 us  [moved(): return lax.ppermute(value, 'seq', pairs)]
    ppermute x2 -> x8, starting transfers between devices: 1.66 us -> 18.3 us  [per_device(): got = lax.ppermute(value, ('seq', 'head'), pairs)]
    unnamed x30 -> x70, local copies, waits for them, and re-layouts: 11.1 us -> 20.4 us
    ppermute x2 -> x8, waiting for transfers between devices: 28 us -> 18.8 us  [per_device(): got = lax.ppermute(value, ('seq', 'head'), pairs)]
  transfers between devices with their start and end apart: 17 -> 23, of which waited for: 12 -> 9; matrix products, arithmetic and copies ran while one was open for 17% -> 6% of each run, Pallas kernels for 7% -> 12%
where the time goes in v2:
time: 529 us; the launch traced here: 528 us
  waiting for transfers between devices  349 us (66%)
  Pallas kernels  64.6 us (12%)
  starting transfers between devices  54.4 us (10%)
  local copies, waits for them, and re-layouts  30.8 us (6%)
  other arithmetic  28.1 us (5%)
    ppermute x9, waiting for transfers between devices, moved(): return lax.ppermute(value, 'seq', pairs)  200 us
    ppermute x6, waiting for transfers between devices, swapped(): return lax.ppermute(value, 'seq', [(s, s ^ 1) for s in range(seq_count)])  131 us
    pallas_call x4, Pallas kernels, project(): pl.pallas_call(partial(project_kernel, depth), grid_spec=pltpu.PrefetchSc...  34.5 us
    ppermute x9, starting transfers between devices, moved(): return lax.ppermute(value, 'seq', pairs)  29.7 us
    pallas_call x1, Pallas kernels, per_device(): pl.pallas_call(partial(local_kernel, per_steps), grid=(heads // STEP_HEAD...  24.5 us
    unnamed x70, local copies, waits for them, and re-layouts  20.4 us
    ppermute x8, waiting for transfers between devices, per_device(): got = lax.ppermute(value, ('seq', 'head'), pairs)  18.8 us
    ppermute x8, starting transfers between devices, per_device(): got = lax.ppermute(value, ('seq', 'head'), pairs)  18.3 us
  transfers between devices with their start and end apart: 23, of which 9 were waited for; matrix products, arithmetic and copies ran while one was open for 6% of the time, Pallas kernels for 12%

profile of v2, /device:TPU:24, one launch (start us, length us, event | category | flops | bytes accessed | tf_op | source)
XLA Modules:
  0.0 527.8 jit_solution(4017473323026390301)
XLA Ops:
  0.0 1.3 collective-permute-start.8
  1.3 6.6 %collective-permute-start.11 = (bf16[4096,512]{1,0:T(8,128)(2,1)}, bf16[4096,512]{1,0:T(8,128)(2,1)}, u32[]{:S(2)}, u32[]{:S(2)}) collective-permute-start(bf16[4096,512]{1,0:T(8,128)(2,1)} %refs_5_.1), channel_id=1, source_target_pairs={{8,0},{12,4},{16,8},{20,12},{24,16},{28,20},{9,1},{13,5},{17,9},{2... | collective-permute-start | bytes 12582920 | tf_op jit(solution)/shard_map/ppermute | solution.py:236
  8.6 1.0 slice.42
  10.3 3.4 collective-permute-start
  14.3 1.1 copy_bitcast_fusion
  15.4 1.2 reduce-window.20
  21.1 1.6 multiply_bitcast_fusion.col_ref
  26.2 72.8 %collective-permute-done = bf16[16,5120]{1,0:T(8,128)(2,1)} collective-permute-done((bf16[16,5120]{1,0:T(8,128)(2,1)}, bf16[16,5120]{1,0:T(8,128)(2,1)}, u32[]{:S(2)}, u32[]{:S(2)}) %collective-permute-start) | collective-permute-done | bytes 163872 | tf_op jit(solution)/shard_map/ppermute | solution.py:236
  99.0 0.9 slice.56.xh_ref
  100.6 1.6 copy-done.7
  102.2 2.2 copy-done.8
  104.4 1.2 copy-done.11
  108.6 24.5 %local_scan.1 = (bf16[512,4096]{1,0:T(8,128)(2,1)S(1)}, bf16[4096,256]{1,0:T(8,128)(2,1)S(1)}, bf16[512,512]{1,0:T(8,128)(2,1)S(1)}) custom-call(bf16[512,4096]{1,0:T(8,128)(2,1)S(1)} %copy-done.8, bf16[16,4096]{1,0:T(8,128)(2,1)S(1)} %slice.56.xh_ref, f32[4,4096]{1,0:T(4,128)S(1)} %copy-done.12, f32[1,4096]{1,0:T(1,128)S(1)} %bitcast.42, ...), custom_call_target="tpu_custom_call" | custom-call | flops 1000000 | bytes 1000000 | tf_op jit(solution)/shard_map/local_scan/pallas_call | solution.py:272
  133.1 2.0 copy-done.5
  135.9 1.0 constant_dynamic-slice_fusion
  137.0 2.0 collective-permute-start.1
  139.0 22.3 %collective-permute-done.1 = f32[64]{0:T(128)S(1)} collective-permute-done((f32[64]{0:T(128)S(1)}, f32[64]{0:T(128)S(1)}, u32[]{:S(2)}, u32[]{:S(2)}) %collective-permute-start.1) | collective-permute-done | bytes 288 | tf_op jit(solution)/shard_map/ppermute | solution.py:232
  161.5 1.3 collective-permute-start.9
  162.8 6.6 %collective-permute-start.14 = (bf16[4096,512]{1,0:T(8,128)(2,1)}, bf16[4096,512]{1,0:T(8,128)(2,1)}, u32[]{:S(2)}, u32[]{:S(2)}) collective-permute-start(bf16[4096,512]{1,0:T(8,128)(2,1)} %collective-permute-done.11.refs_5_), channel_id=1, source_target_pairs={{8,0},{12,4},{16,8},{20,12},{24,16},{28,20},{9,1},{13,5},{17,9},{2... | collective-permute-start | bytes 12582920 | tf_op jit(solution)/shard_map/ppermute | solution.py:236
  169.4 1.5 fusion.1
  170.9 1.3 collective-permute-start.3
  172.4 104.2 %collective-permute-done.3 = bf16[2048,256]{1,0:T(8,128)(2,1)} collective-permute-done((bf16[2048,256]{1,0:T(8,128)(2,1)}, bf16[2048,256]{1,0:T(8,128)(2,1)}, u32[]{:S(2)}, u32[]{:S(2)}) %collective-permute-start.3) | collective-permute-done | bytes 1048608 | tf_op jit(solution)/shard_map/ppermute | solution.py:236
  276.6 1.9 add_convert_fusion.9
  278.6 1.4 collective-permute-start.4
  280.0 22.7 %collective-permute-done.4 = bf16[2048,256]{1,0:T(8,128)(2,1)S(1)} collective-permute-done((bf16[2048,256]{1,0:T(8,128)(2,1)S(1)}, bf16[2048,256]{1,0:T(8,128)(2,1)S(1)}, u32[]{:S(2)}, u32[]{:S(2)}) %collective-permute-start.4) | collective-permute-done | bytes 1048608 | tf_op jit(solution)/shard_map/ppermute | solution.py:236
  302.7 1.5 broadcast_select_fusion.2
  305.1 1.3 collective-permute-start.10
  306.5 1.0 copy.62
  307.5 1.3 reduce-precision_convert_fusion
  308.8 6.5 %collective-permute-start.17 = (bf16[4096,512]{1,0:T(8,128)(2,1)}, bf16[4096,512]{1,0:T(8,128)(2,1)}, u32[]{:S(2)}, u32[]{:S(2)}) collective-permute-start(bf16[4096,512]{1,0:T(8,128)(2,1)} %collective-permute-done.14.refs_5_), channel_id=1, source_target_pairs={{8,0},{12,4},{16,8},{20,12},{24,16},{28,20},{9,1},{13,5},{17,9},{2... | collective-permute-start | bytes 12582920 | tf_op jit(solution)/shard_map/ppermute | solution.py:236
  315.5 10.3 %collective-permute-done.5 = bf16[2048,256]{1,0:T(8,128)(2,1)} collective-permute-done((bf16[2048,256]{1,0:T(8,128)(2,1)}, bf16[2048,256]{1,0:T(8,128)(2,1)}, u32[]{:S(2)}, u32[]{:S(2)}) %collective-permute-start.5) | collective-permute-done | bytes 1048608 | tf_op jit(solution)/shard_map/ppermute | solution.py:232
  325.8 2.2 broadcast_select_fusion.1
  328.4 1.9 copy-done.4
  330.3 2.8 gated_norm.2.refs_0_
  333.1 2.8 gated_norm.3.refs_1_
  336.0 1.2 collective-permute-start.6
  337.2 0.9 collective-permute-start.7
  338.1 46.5 %collective-permute-done.6.refs_2_ = bf16[512,2048]{1,0:T(8,128)(2,1)S(1)} collective-permute-done((bf16[512,2048]{1,0:T(8,128)(2,1)S(1)}, bf16[512,2048]{1,0:T(8,128)(2,1)S(1)}, u32[]{:S(2)}, u32[]{:S(2)}) %collective-permute-start.6) | collective-permute-done | bytes 2097184 | tf_op jit(solution)/shard_map/ppermute | solution.py:232
  384.6 39.1 %collective-permute-done.7.refs_3_ = bf16[512,2048]{1,0:T(8,128)(2,1)S(1)} collective-permute-done((bf16[512,2048]{1,0:T(8,128)(2,1)S(1)}, bf16[512,2048]{1,0:T(8,128)(2,1)S(1)}, u32[]{:S(2)}, u32[]{:S(2)}) %collective-permute-start.7) | collective-permute-done | bytes 2097184 | tf_op jit(solution)/shard_map/ppermute | solution.py:232
  423.7 1.4 copy-done.17
  425.1 8.3 %project.7 = bf16[1024,512]{1,0:T(8,128)(2,1)S(1)} custom-call(s32[1]{0:T(128)} %constant.76.clone.1.first_ref, bf16[512,2048]{1,0:T(8,128)(2,1)S(1)} %gated_norm.2.refs_0_, bf16[512,2048]{1,0:T(8,128)(2,1)S(1)} %gated_norm.3.refs_1_, bf16[512,2048]{1,0:T(8,128)(2,1)} %copy-done.16, bf16[512,2048]{1,0:T(8,128)(2,1)} %copy-done.17, ...), custom_call_target="tpu_custom_call" | custom-call | flops 1000000 | bytes 1000000 | tf_op jit(solution)/shard_map/project/pallas_call | solution.py:179
  433.4 2.3 collective-permute-start.20
  435.7 1.6 copy-done.1
  437.3 9.0 %project.5 = bf16[1024,512]{1,0:T(8,128)(2,1)} custom-call(s32[1]{0:T(128)} %bitcast.12.first_ref, bf16[512,2048]{1,0:T(8,128)(2,1)S(1)} %gated_norm.2.refs_0_, bf16[512,2048]{1,0:T(8,128)(2,1)S(1)} %copy-done.1, bf16[512,2048]{1,0:T(8,128)(2,1)} %copy-done.16, bf16[512,2048]{1,0:T(8,128)(2,1)} %copy-done.17, ...), custom_call_target="tpu_custom_call" | custom-call | flops 1000000 | bytes 1000000 | tf_op jit(solution)/shard_map/project/pallas_call | solution.py:179
  446.3 2.3 collective-permute-start.15
  448.6 1.6 copy-done.2
  450.2 9.0 %project.4 = bf16[1024,512]{1,0:T(8,128)(2,1)} custom-call(s32[1]{0:T(128)} %bitcast.first_ref, bf16[512,2048]{1,0:T(8,128)(2,1)S(1)} %gated_norm.2.refs_0_, bf16[512,2048]{1,0:T(8,128)(2,1)S(1)} %copy-done.2, bf16[512,2048]{1,0:T(8,128)(2,1)} %copy-done.16, bf16[512,2048]{1,0:T(8,128)(2,1)} %copy-done.17, ...), custom_call_target="tpu_custom_call" | custom-call | flops 1000000 | bytes 1000000 | tf_op jit(solution)/shard_map/project/pallas_call | solution.py:179
  459.2 1.3 collective-permute-start.12
  460.5 1.6 copy-done.3
  462.1 8.3 %project.6 = bf16[1024,512]{1,0:T(8,128)(2,1)S(1)} custom-call(s32[1]{0:T(128)} %bitcast.13.first_ref, bf16[512,2048]{1,0:T(8,128)(2,1)S(1)} %gated_norm.2.refs_0_, bf16[512,2048]{1,0:T(8,128)(2,1)S(1)} %copy-done.3, bf16[512,2048]{1,0:T(8,128)(2,1)} %copy-done.16, bf16[512,2048]{1,0:T(8,128)(2,1)} %copy-done.17, ...), custom_call_target="tpu_custom_call" | custom-call | flops 1000000 | bytes 1000000 | tf_op jit(solution)/shard_map/project/pallas_call | solution.py:179
  470.3 1.3 collective-permute-start.18
  471.7 1.5 add_convert_fusion.1
  473.2 1.7 collective-permute-start.21
  474.8 1.8 add_convert_fusion.5
  476.7 1.7 collective-permute-start.16
  478.4 1.8 add_convert_fusion.7
  480.2 1.3 collective-permute-start.13
  481.5 1.3 add_convert_fusion.3
  482.7 6.5 %collective-permute-start.19 = (bf16[1024,512]{1,0:T(8,128)(2,1)}, bf16[1024,512]{1,0:T(8,128)(2,1)}, u32[]{:S(2)}, u32[]{:S(2)}) collective-permute-start(bf16[1024,512]{1,0:T(8,128)(2,1)} %add_convert_fusion.3), channel_id=1, source_target_pairs={{1,3},{5,7},{10,8},{14,12},{19,17},{23,21},{24,26},{28,30}} | collective-permute-start | bytes 3145736 | tf_op jit(solution)/shard_map/ppermute | solution.py:400
  489.2 18.8 %collective-permute-done.13 = bf16[1024,512]{1,0:T(8,128)(2,1)} collective-permute-done((bf16[1024,512]{1,0:T(8,128)(2,1)S(1)}, bf16[1024,512]{1,0:T(8,128)(2,1)}, u32[]{:S(2)}, u32[]{:S(2)}) %collective-permute-start.13) | collective-permute-done | bytes 1048608 | tf_op jit(solution)/shard_map/ppermute | solution.py:400
  508.0 3.6 fusion.3
  511.7 1.5 collective-permute-start.22
  513.1 12.5 %collective-permute-done.22 = bf16[1,512,512]{2,1,0:T(8,128)(2,1)S(1)} collective-permute-done((bf16[1,512,512]{2,1,0:T(8,128)(2,1)S(1)}, bf16[1,512,512]{2,1,0:T(8,128)(2,1)S(1)}, u32[]{:S(2)}, u32[]{:S(2)}) %collective-permute-start.22) | collective-permute-done | bytes 524320 | tf_op jit(solution)/shard_map/ppermute | solution.py:232
  526.5 1.3 copy.65
  (131 shorter events, 17.2 us)
Async XLA Ops:
  0.0 161.5 %collective-permute-start.8 = (bf16[4096,512]{1,0:T(8,128)(2,1)}, bf16[4096,512]{1,0:T(8,128)(2,1)}, u32[]{:S(2)}, u32[]{:S(2)}) collective-permute-start(bf16[4096,512]{1,0:T(8,128)(2,1)} %refs_5_.1), channel_id=1, source_target_pairs={{0,8},{4,12},{8,16},{12,20},{16,24},{20,28},{1,9},{5,13},{9,17},{1... | collective-permute-start | bytes 12582920 | tf_op jit(solution)/shard_map/ppermute | solution.py:236
  1.3 161.5 %collective-permute-start.11 = (bf16[4096,512]{1,0:T(8,128)(2,1)}, bf16[4096,512]{1,0:T(8,128)(2,1)}, u32[]{:S(2)}, u32[]{:S(2)}) collective-permute-start(bf16[4096,512]{1,0:T(8,128)(2,1)} %refs_5_.1), channel_id=1, source_target_pairs={{8,0},{12,4},{16,8},{20,12},{24,16},{28,20},{9,1},{13,5},{17,9},{2... | collective-permute-start | bytes 12582920 | tf_op jit(solution)/shard_map/ppermute | solution.py:236
  8.6 9.7 %copy-start.34 = (s32[4]{0:T(128)S(1)}, s32[4]{0:T(128)}, u32[]{:S(2)}) copy-start(s32[4]{0:T(128)} %param.27) | copy-start | bytes 52
  8.6 11.3 %copy-start.20 = (f32[64,512]{1,0:T(8,128)S(1)}, f32[64,512]{1,0:T(8,128)}, u32[]{:S(2)}) copy-start(f32[64,512]{1,0:T(8,128)} %param.21) | copy-start | bytes 393220
  8.6 11.3 %copy-start.29 = (f32[64]{0:T(128)S(1)}, f32[64]{0:T(128)}, u32[]{:S(2)}) copy-start(f32[64]{0:T(128)} %param.22) | copy-start | bytes 772
  10.3 88.7 %collective-permute-start = (bf16[16,5120]{1,0:T(8,128)(2,1)}, bf16[16,5120]{1,0:T(8,128)(2,1)}, u32[]{:S(2)}, u32[]{:S(2)}) collective-permute-start(bf16[16,5120]{1,0:T(8,128)(2,1)} %pad_maximum_fusion.2), channel_id=1, source_target_pairs={{0,4},{4,8},{8,12},{12,16},{16,20},{20,24},{24,28},{1,5},{5,9},{9,... | collective-permute-start | bytes 491528 | tf_op jit(solution)/shard_map/ppermute | solution.py:236
  17.0 0.7 copy-start.21
  20.0 2.8 copy-start.23
  20.3 0.6 copy-start.30
  21.1 1.7 copy-start.25
  21.1 2.4 copy-start.26
  21.1 2.9 copy-start.27
  21.1 3.5 copy-start.32
  21.1 4.8 copy-start.33
  100.6 1.6 copy-start.7
  102.2 2.2 copy-start.8
  104.4 1.2 copy-start.11
  105.6 0.8 copy-start.12
  106.5 0.7 copy-start.13
  107.2 0.7 copy-start.14
  107.9 0.7 copy-start.15
  133.1 2.1 copy-start.5
  135.1 0.8 copy-start.9
  135.9 1.0 copy-start.31
  137.0 32.5 %collective-permute-start.2 = (bf16[2048,256]{1,0:T(8,128)(2,1)}, bf16[2048,256]{1,0:T(8,128)(2,1)S(1)}, u32[]{:S(2)}, u32[]{:S(2)}) collective-permute-start(bf16[2048,256]{1,0:T(8,128)(2,1)} %constant_dynamic-slice_fusion), channel_id=1, source_target_pairs={{0,4},{4,0},{8,12},{12,8},{16,20},{20,16},{24,28},{28,24},{1,5},{5... | collective-permute-start | bytes 3145736 | tf_op jit(solution)/shard_map/ppermute | solution.py:232
  137.0 24.3 %collective-permute-start.1 = (f32[64]{0:T(128)S(1)}, f32[64]{0:T(128)S(1)}, u32[]{:S(2)}, u32[]{:S(2)}) collective-permute-start(f32[64]{0:T(128)S(1)} %exp.20), channel_id=1, source_target_pairs={{0,4},{4,0},{8,12},{12,8},{16,20},{20,16},{24,28},{28,24},{1,5},{5... | collective-permute-start | bytes 776 | tf_op jit(solution)/shard_map/ppermute | solution.py:232
  161.5 143.6 %collective-permute-start.9 = (bf16[4096,512]{1,0:T(8,128)(2,1)}, bf16[4096,512]{1,0:T(8,128)(2,1)}, u32[]{:S(2)}, u32[]{:S(2)}) collective-permute-start(bf16[4096,512]{1,0:T(8,128)(2,1)} %collective-permute-done.8.refs_4_), channel_id=1, source_target_pairs={{0,8},{4,12},{8,16},{12,20},{16,24},{20,28},{1,9},{5,13},{9,17},{1... | collective-permute-start | bytes 12582920 | tf_op jit(solution)/shard_map/ppermute | solution.py:236
  162.8 146.0 %collective-permute-start.14 = (bf16[4096,512]{1,0:T(8,128)(2,1)}, bf16[4096,512]{1,0:T(8,128)(2,1)}, u32[]{:S(2)}, u32[]{:S(2)}) collective-permute-start(bf16[4096,512]{1,0:T(8,128)(2,1)} %collective-permute-done.11.refs_5_), channel_id=1, source_target_pairs={{8,0},{12,4},{16,8},{20,12},{24,16},{28,20},{9,1},{13,5},{17,9},{2... | collective-permute-start | bytes 12582920 | tf_op jit(solution)/shard_map/ppermute | solution.py:236
  170.9 105.7 %collective-permute-start.3 = (bf16[2048,256]{1,0:T(8,128)(2,1)}, bf16[2048,256]{1,0:T(8,128)(2,1)}, u32[]{:S(2)}, u32[]{:S(2)}) collective-permute-start(bf16[2048,256]{1,0:T(8,128)(2,1)} %fusion.1), channel_id=1, source_target_pairs={{0,8},{4,12},{8,16},{12,20},{16,24},{20,28},{1,9},{5,13},{9,17},{1... | collective-permute-start | bytes 3145736 | tf_op jit(solution)/shard_map/ppermute | solution.py:236
  278.5 27.8 %copy-start.22 = (f32[64,4,128]{2,1,0:T(4,128)S(1)}, f32[64,4,128]{2,1,0:T(4,128)}, u32[]{:S(2)}) copy-start(f32[64,4,128]{2,1,0:T(4,128)} %copy-done.21) | copy-start | bytes 393220
  278.6 28.9 %copy-start.28 = (bf16[4096]{0:T(1024)(128)(2,1)S(1)}, bf16[4096]{0:T(1024)(128)(2,1)}, u32[]{:S(2)}) copy-start(bf16[4096]{0:T(1024)(128)(2,1)} %param.25) | copy-start | bytes 24580
  278.6 28.9 %copy-start.24 = (f32[512]{0:T(512)S(1)}, f32[512]{0:T(512)}, u32[]{:S(2)}) copy-start(f32[512]{0:T(512)} %copy-done.23) | copy-start | bytes 6148
  278.6 24.1 %collective-permute-start.4 = (bf16[2048,256]{1,0:T(8,128)(2,1)S(1)}, bf16[2048,256]{1,0:T(8,128)(2,1)S(1)}, u32[]{:S(2)}, u32[]{:S(2)}) collective-permute-start(bf16[2048,256]{1,0:T(8,128)(2,1)S(1)} %add_convert_fusion.9), channel_id=1, source_target_pairs={{0,8},{4,12},{8,16},{12,20},{16,24},{20,28},{1,9},{5,13},{9,17},{1... | collective-permute-start | bytes 3145736 | tf_op jit(solution)/shard_map/ppermute | solution.py:236
  302.7 1.5 copy-start.18
  304.2 21.5 %collective-permute-start.5 = (bf16[2048,256]{1,0:T(8,128)(2,1)}, bf16[2048,256]{1,0:T(8,128)(2,1)}, u32[]{:S(2)}, u32[]{:S(2)}) collective-permute-start(bf16[2048,256]{1,0:T(8,128)(2,1)} %broadcast_select_fusion.2), channel_id=1, source_target_pairs={{0,4},{4,0},{8,12},{12,8},{16,20},{20,16},{24,28},{28,24},{1,5},{5... | collective-permute-start | bytes 3145736 | tf_op jit(solution)/shard_map/ppermute | solution.py:232
  305.1 143.5 %collective-permute-start.10 = (bf16[4096,512]{1,0:T(8,128)(2,1)}, bf16[4096,512]{1,0:T(8,128)(2,1)}, u32[]{:S(2)}, u32[]{:S(2)}) collective-permute-start(bf16[4096,512]{1,0:T(8,128)(2,1)} %collective-permute-done.9.refs_4_), channel_id=1, source_target_pairs={{0,8},{4,12},{8,16},{12,20},{16,24},{20,28},{1,9},{5,13},{9,17},{1... | collective-permute-start | bytes 12582920 | tf_op jit(solution)/shard_map/ppermute | solution.py:236
  307.5 18.3 %copy-start.19 = (bf16[2048,256]{1,0:T(8,128)(2,1)S(1)}, bf16[2048,256]{1,0:T(8,128)(2,1)}, u32[]{:S(2)}) copy-start(bf16[2048,256]{1,0:T(8,128)(2,1)} %copy-done.18) | copy-start | bytes 3145732
  308.8 151.6 %collective-permute-start.17 = (bf16[4096,512]{1,0:T(8,128)(2,1)}, bf16[4096,512]{1,0:T(8,128)(2,1)}, u32[]{:S(2)}, u32[]{:S(2)}) collective-permute-start(bf16[4096,512]{1,0:T(8,128)(2,1)} %collective-permute-done.14.refs_5_), channel_id=1, source_target_pairs={{8,0},{12,4},{16,8},{20,12},{24,16},{28,20},{9,1},{13,5},{17,9},{2... | collective-permute-start | bytes 12582920 | tf_op jit(solution)/shard_map/ppermute | solution.py:236
  325.7 2.5 copy-start.6
  325.8 2.6 copy-start.10
  328.0 2.3 copy-start.4
  336.0 97.5 %copy-start = (bf16[512,2048]{1,0:T(8,128)(2,1)}, bf16[512,2048]{1,0:T(8,128)(2,1)S(1)}, u32[]{:S(2)}) copy-start(bf16[512,2048]{1,0:T(8,128)(2,1)S(1)} %gated_norm.3.refs_1_) | copy-start | bytes 6291460
  336.0 48.6 %collective-permute-start.6 = (bf16[512,2048]{1,0:T(8,128)(2,1)S(1)}, bf16[512,2048]{1,0:T(8,128)(2,1)S(1)}, u32[]{:S(2)}, u32[]{:S(2)}) collective-permute-start(bf16[512,2048]{1,0:T(8,128)(2,1)S(1)} %gated_norm.2.refs_0_), channel_id=1, source_target_pairs={{0,4},{4,0},{8,12},{12,8},{16,20},{20,16},{24,28},{28,24},{1,5},{5... | collective-permute-start | bytes 6291464 | tf_op jit(solution)/shard_map/ppermute | solution.py:232
  337.2 86.5 %collective-permute-start.7 = (bf16[512,2048]{1,0:T(8,128)(2,1)S(1)}, bf16[512,2048]{1,0:T(8,128)(2,1)S(1)}, u32[]{:S(2)}, u32[]{:S(2)}) collective-permute-start(bf16[512,2048]{1,0:T(8,128)(2,1)S(1)} %gated_norm.3.refs_1_), channel_id=1, source_target_pairs={{0,4},{4,0},{8,12},{12,8},{16,20},{20,16},{24,28},{28,24},{1,5},{5... | collective-permute-start | bytes 6291464 | tf_op jit(solution)/shard_map/ppermute | solution.py:232
  384.6 39.1 %copy-start.16 = (bf16[512,2048]{1,0:T(8,128)(2,1)}, bf16[512,2048]{1,0:T(8,128)(2,1)S(1)}, u32[]{:S(2)}) copy-start(bf16[512,2048]{1,0:T(8,128)(2,1)S(1)} %collective-permute-done.6.refs_2_) | copy-start | bytes 6291460
  423.7 1.4 copy-start.17
  433.4 38.2 %collective-permute-start.20 = (bf16[1024,512]{1,0:T(8,128)(2,1)S(1)}, bf16[1024,512]{1,0:T(8,128)(2,1)}, u32[]{:S(2)}, u32[]{:S(2)}) collective-permute-start(bf16[1024,512]{1,0:T(8,128)(2,1)S(1)} %project.7), channel_id=1, source_target_pairs={{1,0},{3,2},{5,4},{7,6},{8,9},{10,11},{12,13},{14,15},{17,16},{19,... | collective-permute-start | bytes 3145736 | tf_op jit(solution)/shard_map/ppermute | solution.py:400
  435.7 1.6 copy-start.1
  446.3 28.5 %collective-permute-start.15 = (bf16[1024,512]{1,0:T(8,128)(2,1)}, bf16[1024,512]{1,0:T(8,128)(2,1)}, u32[]{:S(2)}, u32[]{:S(2)}) collective-permute-start(bf16[1024,512]{1,0:T(8,128)(2,1)} %project.5), channel_id=1, source_target_pairs={{1,0},{3,2},{5,4},{7,6},{8,9},{10,11},{12,13},{14,15},{17,16},{19,... | collective-permute-start | bytes 3145736 | tf_op jit(solution)/shard_map/ppermute | solution.py:400
  448.6 1.6 copy-start.2
  459.2 19.2 %collective-permute-start.12 = (bf16[1024,512]{1,0:T(8,128)(2,1)}, bf16[1024,512]{1,0:T(8,128)(2,1)}, u32[]{:S(2)}, u32[]{:S(2)}) collective-permute-start(bf16[1024,512]{1,0:T(8,128)(2,1)} %project.4), channel_id=1, source_target_pairs={{0,1},{2,3},{4,5},{6,7},{9,8},{11,10},{13,12},{15,14},{16,17},{18,... | collective-permute-start | bytes 3145736 | tf_op jit(solution)/shard_map/ppermute | solution.py:400
  460.5 1.6 copy-start.3
  470.3 11.1 %collective-permute-start.18 = (bf16[1024,512]{1,0:T(8,128)(2,1)S(1)}, bf16[1024,512]{1,0:T(8,128)(2,1)S(1)}, u32[]{:S(2)}, u32[]{:S(2)}) collective-permute-start(bf16[1024,512]{1,0:T(8,128)(2,1)S(1)} %project.6), channel_id=1, source_target_pairs={{0,1},{2,3},{4,5},{6,7},{9,8},{11,10},{13,12},{15,14},{16,17},{18,... | collective-permute-start | bytes 3145736 | tf_op jit(solution)/shard_map/ppermute | solution.py:400
  473.2 16.1 %collective-permute-start.21 = (bf16[1024,512]{1,0:T(8,128)(2,1)S(1)}, bf16[1024,512]{1,0:T(8,128)(2,1)}, u32[]{:S(2)}, u32[]{:S(2)}) collective-permute-start(bf16[1024,512]{1,0:T(8,128)(2,1)S(1)} %add_convert_fusion.1), channel_id=1, source_target_pairs={{2,0},{6,4},{11,9},{15,13},{16,18},{20,22},{25,27},{29,31}} | collective-permute-start | bytes 3145736 | tf_op jit(solution)/shard_map/ppermute | solution.py:400
  476.7 12.6 %collective-permute-start.16 = (bf16[1024,512]{1,0:T(8,128)(2,1)S(1)}, bf16[1024,512]{1,0:T(8,128)(2,1)}, u32[]{:S(2)}, u32[]{:S(2)}) collective-permute-start(bf16[1024,512]{1,0:T(8,128)(2,1)S(1)} %add_convert_fusion.5), channel_id=1, source_target_pairs={{0,2},{4,6},{9,11},{13,15},{18,16},{22,20},{27,25},{31,29}} | collective-permute-start | bytes 3145736 | tf_op jit(solution)/shard_map/ppermute | solution.py:400
  480.2 27.8 %collective-permute-start.13 = (bf16[1024,512]{1,0:T(8,128)(2,1)S(1)}, bf16[1024,512]{1,0:T(8,128)(2,1)}, u32[]{:S(2)}, u32[]{:S(2)}) collective-permute-start(bf16[1024,512]{1,0:T(8,128)(2,1)S(1)} %add_convert_fusion.7), channel_id=1, source_target_pairs={{3,1},{7,5},{8,10},{12,14},{17,19},{21,23},{26,24},{30,28}} | collective-permute-start | bytes 3145736 | tf_op jit(solution)/shard_map/ppermute | solution.py:400
  482.7 25.3 %collective-permute-start.19 = (bf16[1024,512]{1,0:T(8,128)(2,1)}, bf16[1024,512]{1,0:T(8,128)(2,1)}, u32[]{:S(2)}, u32[]{:S(2)}) collective-permute-start(bf16[1024,512]{1,0:T(8,128)(2,1)} %add_convert_fusion.3), channel_id=1, source_target_pairs={{1,3},{5,7},{10,8},{14,12},{19,17},{23,21},{24,26},{28,30}} | collective-permute-start | bytes 3145736 | tf_op jit(solution)/shard_map/ppermute | solution.py:400
  511.7 14.0 %collective-permute-start.22 = (bf16[1,512,512]{2,1,0:T(8,128)(2,1)S(1)}, bf16[1,512,512]{2,1,0:T(8,128)(2,1)S(1)}, u32[]{:S(2)}, u32[]{:S(2)}) collective-permute-start(bf16[1,512,512]{2,1,0:T(8,128)(2,1)S(1)} %slice.61), channel_id=1, source_target_pairs={{0,4},{4,0},{8,12},{12,8},{16,20},{20,16},{24,28},{28,24},{1,5},{5... | collective-permute-start | bytes 1572872 | tf_op jit(solution)/shard_map/ppermute | solution.py:232

commit v3 on v2

--- a/solution.py
+++ b/solution.py
@@ -235,14 +235,14 @@
         pairs = [(s, s + by) for s in range(seq_count) if 0 <= s + by < seq_count]
         return lax.ppermute(value, "seq", pairs)
 
-    up, down = [out_weight], [out_weight]
-    for _ in range(rows_count - 1):
-        up.append(moved(up[-1], 2))
-        down.append(moved(down[-1], -2))
-
     halo = moved(
         jnp.concatenate([inner_input[tokens - HALO :], state_input[tokens - HALO :]], axis=1), 1
     )
+    first_weight, halo = lax.optimization_barrier((out_weight, halo))
+    up, down = [out_weight], [out_weight]
+    if rows_count > 1:
+        up.append(moved(first_weight, 2))
+        down.append(moved(first_weight, -2))
     positions = seq_at * tokens + lax.iota(jnp.int32, tokens + 3) - 3
     seg_extended = segment_of(positions, sequence_lengths)
     seg = seg_extended[3:]
@@ -345,6 +345,10 @@
     for hop in range(max(1, seq_count // 4)):
         arriving = moved(window.astype(BF16), 2).astype(F32)
         window = pair_total + pair_factor * arriving
+    up[-1], down[-1], arriving = lax.optimization_barrier((up[-1], down[-1], arriving))
+    if rows_count > 2:
+        up.append(moved(up[-1], 2))
+        down.append(moved(down[-1], -2))
     after_first = (first_factor * arriving + first_end).astype(BF16)
     arriving = arriving.astype(BF16)
     own_part = jnp.where(side == 0, arriving, after_first)
@@ -379,6 +383,12 @@
         own.append(normed)
         peer.append(swapped(normed))
     acts = own + peer
+    zero = (own[-1][:16, :128] + peer[0][:16, :128]) * jnp.zeros((), BF16)
+    up[-1] = lax.dynamic_update_slice(up[-1], up[-1][:16, :128] + zero, (0, 0))
+    down[-1] = lax.dynamic_update_slice(down[-1], down[-1][:16, :128] + zero, (0, 0))
+    for _ in range(rows_count - 3):
+        up.append(moved(up[-1], 2))
+        down.append(moved(down[-1], -2))
 
     per_head = rows_count // head_count
     reduced = []

time: 529 us -> 437 us (0.83)
  waiting for transfers between devices: 349 us -> 257 us
    ppermute x9, waiting for transfers between devices: 200 us -> 105 us  [moved(): return lax.ppermute(value, 'seq', pairs)]
    unnamed x70 -> x66, local copies, waits for them, and re-layouts: 20.4 us -> 19 us
  transfers between devices with their start and end apart: 23 -> 23, of which waited for: 9 -> 11; matrix products, arithmetic and copies ran while one was open for 6% -> 7% of each run, Pallas kernels for 12% -> 15%
where the time goes in v3:
time: 437 us; the launch traced here: 435 us
  waiting for transfers between devices  257 us (59%)
  Pallas kernels  64.6 us (15%)
  starting transfers between devices  50.4 us (12%)
  other arithmetic  33.1 us (8%)
  local copies, waits for them, and re-layouts  29.5 us (7%)
    ppermute x6, waiting for transfers between devices, swapped(): return lax.ppermute(value, 'seq', [(s, s ^ 1) for s in range(seq_count)])  133 us
    ppermute x9, waiting for transfers between devices, moved(): return lax.ppermute(value, 'seq', pairs)  105 us
    pallas_call x4, Pallas kernels, project(): pl.pallas_call(partial(project_kernel, depth), grid_spec=pltpu.PrefetchSc...  34.5 us
    ppermute x9, starting transfers between devices, moved(): return lax.ppermute(value, 'seq', pairs)  28.4 us
    pallas_call x1, Pallas kernels, per_device(): pl.pallas_call(partial(local_kernel, per_steps), grid=(heads // STEP_HEAD...  24.5 us
    unnamed x66, local copies, waits for them, and re-layouts  19 us
    ppermute x8, waiting for transfers between devices, per_device(): got = lax.ppermute(value, ('seq', 'head'), pairs)  18.8 us
    ppermute x8, starting transfers between devices, per_device(): got = lax.ppermute(value, ('seq', 'head'), pairs)  18.3 us
  transfers between devices with their start and end apart: 23, of which 11 were waited for; matrix products, arithmetic and copies ran while one was open for 7% of the time, Pallas kernels for 15%

profile of v3, /device:TPU:24, one launch (start us, length us, event | category | flops | bytes accessed | tf_op | source)
XLA Modules:
  0.0 435.2 jit_solution(12748661109471692060)
XLA Ops:
  0.8 0.9 slice.54
  2.4 3.4 collective-permute-start
  8.1 1.1 copy_bitcast_fusion
  9.1 1.2 reduce-window.20
  13.0 1.6 multiply_bitcast_fusion.col_ref
  20.1 1.3 collective-permute-start.1
  21.4 6.6 %collective-permute-start.2 = (bf16[4096,512]{1,0:T(8,128)(2,1)}, bf16[4096,512]{1,0:T(8,128)(2,1)}, u32[]{:S(2)}, u32[]{:S(2)}) collective-permute-start(bf16[4096,512]{1,0:T(8,128)(2,1)} %refs_5_.1), channel_id=1, source_target_pairs={{8,0},{12,4},{16,8},{20,12},{24,16},{28,20},{9,1},{13,5},{17,9},{2... | collective-permute-start | bytes 12582920 | tf_op jit(solution)/shard_map/ppermute | solution.py:236
  28.0 1.6 copy-done.7
  29.6 2.2 copy-done.8
  31.8 1.2 copy-done.11
  36.0 24.5 %local_scan.1 = (bf16[512,4096]{1,0:T(8,128)(2,1)S(1)}, bf16[4096,256]{1,0:T(8,128)(2,1)S(1)}, bf16[512,512]{1,0:T(8,128)(2,1)S(1)}) custom-call(bf16[512,4096]{1,0:T(8,128)(2,1)S(1)} %copy-done.8, bf16[16,4096]{1,0:T(8,128)(2,1)S(1)} %slice.56.xh_ref, f32[4,4096]{1,0:T(4,128)S(1)} %copy-done.12, f32[1,4096]{1,0:T(1,128)S(1)} %bitcast.42, ...), custom_call_target="tpu_custom_call" | custom-call | flops 1000000 | bytes 1000000 | tf_op jit(solution)/shard_map/local_scan/pallas_call | solution.py:272
  60.4 2.0 copy-done.5
  63.3 1.0 constant_dynamic-slice_fusion
  64.4 2.0 collective-permute-start.3
  66.4 22.3 %collective-permute-done.3 = f32[64]{0:T(128)S(1)} collective-permute-done((f32[64]{0:T(128)S(1)}, f32[64]{0:T(128)S(1)}, u32[]{:S(2)}, u32[]{:S(2)}) %collective-permute-start.3) | collective-permute-done | bytes 288 | tf_op jit(solution)/shard_map/ppermute | solution.py:232
  88.9 1.5 fusion.1
  90.4 1.3 collective-permute-start.5
  91.9 44.9 %collective-permute-done.5 = bf16[2048,256]{1,0:T(8,128)(2,1)} collective-permute-done((bf16[2048,256]{1,0:T(8,128)(2,1)}, bf16[2048,256]{1,0:T(8,128)(2,1)}, u32[]{:S(2)}, u32[]{:S(2)}) %collective-permute-start.5) | collective-permute-done | bytes 1048608 | tf_op jit(solution)/shard_map/ppermute | solution.py:236
  136.8 1.9 add_convert_fusion.9
  138.8 1.3 collective-permute-start.6
  140.1 24.3 %collective-permute-done.6 = bf16[2048,256]{1,0:T(8,128)(2,1)S(1)} collective-permute-done((bf16[2048,256]{1,0:T(8,128)(2,1)S(1)}, bf16[2048,256]{1,0:T(8,128)(2,1)S(1)}, u32[]{:S(2)}, u32[]{:S(2)}) %collective-permute-start.6) | collective-permute-done | bytes 1048608 | tf_op jit(solution)/shard_map/ppermute | solution.py:236
  164.6 1.6 broadcast_select_fusion.2
  166.8 5.3 %collective-permute-start.14 = (bf16[4096,512]{1,0:T(8,128)(2,1)}, bf16[4096,512]{1,0:T(8,128)(2,1)}, u32[]{:S(2)}, u32[]{:S(2)}) collective-permute-start(bf16[4096,512]{1,0:T(8,128)(2,1)} %collective-permute-done.2.refs_5_), channel_id=1, source_target_pairs={{8,0},{12,4},{16,8},{20,12},{24,16},{28,20},{9,1},{13,5},{17,9},{2... | collective-permute-start | bytes 12582920 | tf_op jit(solution)/shard_map/ppermute | solution.py:236
  172.0 1.5 collective-permute-start.10
  173.6 1.0 copy.62
  174.6 1.2 reduce-precision_convert_fusion
  176.0 13.3 %collective-permute-done.7 = bf16[2048,256]{1,0:T(8,128)(2,1)} collective-permute-done((bf16[2048,256]{1,0:T(8,128)(2,1)}, bf16[2048,256]{1,0:T(8,128)(2,1)}, u32[]{:S(2)}, u32[]{:S(2)}) %collective-permute-start.7) | collective-permute-done | bytes 1048608 | tf_op jit(solution)/shard_map/ppermute | solution.py:232
  189.3 3.0 broadcast_select_fusion.1
  192.3 1.4 broadcast_select_fusion
  193.9 2.0 copy-done.4
  195.9 2.8 gated_norm.2.refs_0_
  198.9 2.8 gated_norm.3.refs_1_
  201.7 41.5 %collective-permute-done.8.refs_2_ = bf16[512,2048]{1,0:T(8,128)(2,1)S(1)} collective-permute-done((bf16[512,2048]{1,0:T(8,128)(2,1)S(1)}, bf16[512,2048]{1,0:T(8,128)(2,1)S(1)}, u32[]{:S(2)}, u32[]{:S(2)}) %collective-permute-start.8) | collective-permute-done | bytes 2097184 | tf_op jit(solution)/shard_map/ppermute | solution.py:232
  243.2 14.7 %collective-permute-done.14 = bf16[4096,512]{1,0:T(8,128)(2,1)} collective-permute-done((bf16[4096,512]{1,0:T(8,128)(2,1)}, bf16[4096,512]{1,0:T(8,128)(2,1)}, u32[]{:S(2)}, u32[]{:S(2)}) %collective-permute-start.14) | collective-permute-done | bytes 4194336 | tf_op jit(solution)/shard_map/ppermute | solution.py:236
  257.8 6.0 %collective-permute-done.10 = bf16[4096,512]{1,0:T(8,128)(2,1)} collective-permute-done((bf16[4096,512]{1,0:T(8,128)(2,1)}, bf16[4096,512]{1,0:T(8,128)(2,1)}, u32[]{:S(2)}, u32[]{:S(2)}) %collective-permute-start.10) | collective-permute-done | bytes 4194336 | tf_op jit(solution)/shard_map/ppermute | solution.py:236
  263.9 1.3 fusion.8
  265.1 1.3 collective-permute-start.11
  266.4 6.6 %collective-permute-start.17 = (bf16[4096,512]{1,0:T(8,128)(2,1)}, bf16[4096,512]{1,0:T(8,128)(2,1)}, u32[]{:S(2)}, u32[]{:S(2)}) collective-permute-start(bf16[4096,512]{1,0:T(8,128)(2,1)} %get-tuple-element.25.refs_5_), channel_id=1, source_target_pairs={{8,0},{12,4},{16,8},{20,12},{24,16},{28,20},{9,1},{13,5},{17,9},{2... | collective-permute-start | bytes 12582920 | tf_op jit(solution)/shard_map/ppermute | solution.py:236
  273.5 42.7 %collective-permute-done.9.refs_3_ = bf16[512,2048]{1,0:T(8,128)(2,1)S(1)} collective-permute-done((bf16[512,2048]{1,0:T(8,128)(2,1)S(1)}, bf16[512,2048]{1,0:T(8,128)(2,1)S(1)}, u32[]{:S(2)}, u32[]{:S(2)}) %collective-permute-start.9) | collective-permute-done | bytes 2097184 | tf_op jit(solution)/shard_map/ppermute | solution.py:232
  316.2 1.3 copy-done.17
  317.5 8.3 %project.7 = bf16[1024,512]{1,0:T(8,128)(2,1)S(1)} custom-call(s32[1]{0:T(128)} %constant.78.clone.1.first_ref, bf16[512,2048]{1,0:T(8,128)(2,1)S(1)} %gated_norm.2.refs_0_, bf16[512,2048]{1,0:T(8,128)(2,1)S(1)} %gated_norm.3.refs_1_, bf16[512,2048]{1,0:T(8,128)(2,1)} %copy-done.16, bf16[512,2048]{1,0:T(8,128)(2,1)} %copy-done.17, ...), custom_call_target="tpu_custom_call" | custom-call | flops 1000000 | bytes 1000000 | tf_op jit(solution)/shard_map/project/pallas_call | solution.py:179
  325.8 2.3 collective-permute-start.20
  328.1 1.6 copy-done.1
  329.7 9.0 %project.5 = bf16[1024,512]{1,0:T(8,128)(2,1)} custom-call(s32[1]{0:T(128)} %bitcast.12.first_ref, bf16[512,2048]{1,0:T(8,128)(2,1)S(1)} %copy-done.1, bf16[512,2048]{1,0:T(8,128)(2,1)S(1)} %gated_norm.3.refs_1_, bf16[512,2048]{1,0:T(8,128)(2,1)} %copy-done.16, bf16[512,2048]{1,0:T(8,128)(2,1)} %copy-done.17, bf16[4096,512]{1,0:T(8,128)(2,1)} %get-tuple-element.26.refs_4_, ...), custom_call_target="tpu_custom_call" | custom-call | flops 1000000 | bytes 1000000 | tf_op jit(solution)/shard_map/project/pallas_call | solution.py:179
  338.7 2.3 collective-permute-start.15
  341.0 15.0 %collective-permute-done.11.refs_4_ = bf16[4096,512]{1,0:T(8,128)(2,1)} collective-permute-done((bf16[4096,512]{1,0:T(8,128)(2,1)}, bf16[4096,512]{1,0:T(8,128)(2,1)}, u32[]{:S(2)}, u32[]{:S(2)}) %collective-permute-start.11) | collective-permute-done | bytes 4194336 | tf_op jit(solution)/shard_map/ppermute | solution.py:236
  356.1 1.6 copy-done.2
  357.6 9.0 %project.4 = bf16[1024,512]{1,0:T(8,128)(2,1)} custom-call(s32[1]{0:T(128)} %bitcast.first_ref, bf16[512,2048]{1,0:T(8,128)(2,1)S(1)} %copy-done.2, bf16[512,2048]{1,0:T(8,128)(2,1)S(1)} %gated_norm.3.refs_1_, bf16[512,2048]{1,0:T(8,128)(2,1)} %copy-done.16, bf16[512,2048]{1,0:T(8,128)(2,1)} %copy-done.17, ...), custom_call_target="tpu_custom_call" | custom-call | flops 1000000 | bytes 1000000 | tf_op jit(solution)/shard_map/project/pallas_call | solution.py:179
  366.6 1.3 collective-permute-start.12
  367.9 1.6 copy-done.3
  369.5 8.3 %project.6 = bf16[1024,512]{1,0:T(8,128)(2,1)S(1)} custom-call(s32[1]{0:T(128)} %bitcast.13.first_ref, bf16[512,2048]{1,0:T(8,128)(2,1)S(1)} %copy-done.3, bf16[512,2048]{1,0:T(8,128)(2,1)S(1)} %gated_norm.3.refs_1_, bf16[512,2048]{1,0:T(8,128)(2,1)} %copy-done.16, bf16[512,2048]{1,0:T(8,128)(2,1)} %copy-done.17, ...), custom_call_target="tpu_custom_call" | custom-call | flops 1000000 | bytes 1000000 | tf_op jit(solution)/shard_map/project/pallas_call | solution.py:179
  377.8 1.3 collective-permute-start.18
  379.1 1.5 add_convert_fusion.1
  380.6 1.7 collective-permute-start.21
  382.3 1.8 add_convert_fusion.5
  384.1 1.7 collective-permute-start.16
  385.8 1.8 add_convert_fusion.7
  387.6 1.3 collective-permute-start.13
  388.9 1.3 add_convert_fusion.3
  390.2 6.5 %collective-permute-start.19 = (bf16[1024,512]{1,0:T(8,128)(2,1)}, bf16[1024,512]{1,0:T(8,128)(2,1)}, u32[]{:S(2)}, u32[]{:S(2)}) collective-permute-start(bf16[1024,512]{1,0:T(8,128)(2,1)} %add_convert_fusion.3), channel_id=1, source_target_pairs={{1,3},{5,7},{10,8},{14,12},{19,17},{23,21},{24,26},{28,30}} | collective-permute-start | bytes 3145736 | tf_op jit(solution)/shard_map/ppermute | solution.py:410
  396.7 18.8 %collective-permute-done.13 = bf16[1024,512]{1,0:T(8,128)(2,1)} collective-permute-done((bf16[1024,512]{1,0:T(8,128)(2,1)S(1)}, bf16[1024,512]{1,0:T(8,128)(2,1)}, u32[]{:S(2)}, u32[]{:S(2)}) %collective-permute-start.13) | collective-permute-done | bytes 1048608 | tf_op jit(solution)/shard_map/ppermute | solution.py:410
  415.5 3.6 fusion.3
  419.6 13.5 %collective-permute-done.22 = bf16[1,512,512]{2,1,0:T(8,128)(2,1)S(1)} collective-permute-done((bf16[1,512,512]{2,1,0:T(8,128)(2,1)S(1)}, bf16[1,512,512]{2,1,0:T(8,128)(2,1)S(1)}, u32[]{:S(2)}, u32[]{:S(2)}) %collective-permute-start.22) | collective-permute-done | bytes 524320 | tf_op jit(solution)/shard_map/ppermute | solution.py:232
  433.9 1.3 copy.65
  (130 shorter events, 19.1 us)
Async XLA Ops:
  0.8 12.0 %copy-start.19 = (f32[64,512]{1,0:T(8,128)S(1)}, f32[64,512]{1,0:T(8,128)}, u32[]{:S(2)}) copy-start(f32[64,512]{1,0:T(8,128)} %param.21) | copy-start | bytes 393220
  0.8 12.0 %copy-start.28 = (f32[64]{0:T(128)S(1)}, f32[64]{0:T(128)}, u32[]{:S(2)}) copy-start(f32[64]{0:T(128)} %param.22) | copy-start | bytes 772
  2.4 16.0 %collective-permute-start = (bf16[16,5120]{1,0:T(8,128)(2,1)}, bf16[16,5120]{1,0:T(8,128)(2,1)}, u32[]{:S(2)}, u32[]{:S(2)}) collective-permute-start(bf16[16,5120]{1,0:T(8,128)(2,1)} %pad_maximum_fusion.2), channel_id=1, source_target_pairs={{0,4},{4,8},{8,12},{12,16},{16,20},{20,24},{24,28},{1,5},{5,9},{9,... | collective-permute-start | bytes 491528 | tf_op jit(solution)/shard_map/ppermute | solution.py:236
  10.8 1.3 copy-start.20
  12.8 1.8 copy-start.22
  13.0 2.1 copy-start.24
  13.0 2.7 copy-start.25
  13.0 3.3 copy-start.26
  13.0 3.9 copy-start.31
  14.6 3.6 copy-start.32
  14.8 2.9 copy-start.29
  20.1 144.4 %collective-permute-start.1 = (bf16[4096,512]{1,0:T(8,128)(2,1)}, bf16[4096,512]{1,0:T(8,128)(2,1)}, u32[]{:S(2)}, u32[]{:S(2)}) collective-permute-start(bf16[4096,512]{1,0:T(8,128)(2,1)} %refs_5_.1), channel_id=1, source_target_pairs={{0,8},{4,12},{8,16},{12,20},{16,24},{20,28},{1,9},{5,13},{9,17},{1... | collective-permute-start | bytes 12582920 | tf_op jit(solution)/shard_map/ppermute | solution.py:236
  21.4 143.2 %collective-permute-start.2 = (bf16[4096,512]{1,0:T(8,128)(2,1)}, bf16[4096,512]{1,0:T(8,128)(2,1)}, u32[]{:S(2)}, u32[]{:S(2)}) collective-permute-start(bf16[4096,512]{1,0:T(8,128)(2,1)} %refs_5_.1), channel_id=1, source_target_pairs={{8,0},{12,4},{16,8},{20,12},{24,16},{28,20},{9,1},{13,5},{17,9},{2... | collective-permute-start | bytes 12582920 | tf_op jit(solution)/shard_map/ppermute | solution.py:236
  28.0 1.6 copy-start.7
  29.6 2.2 copy-start.8
  31.8 1.2 copy-start.11
  33.0 0.8 copy-start.12
  33.9 0.7 copy-start.13
  34.6 0.7 copy-start.14
  35.3 0.7 copy-start.15
  60.4 2.0 copy-start.5
  62.5 0.8 copy-start.9
  63.3 1.0 copy-start.30
  64.4 24.6 %collective-permute-start.4 = (bf16[2048,256]{1,0:T(8,128)(2,1)}, bf16[2048,256]{1,0:T(8,128)(2,1)S(1)}, u32[]{:S(2)}, u32[]{:S(2)}) collective-permute-start(bf16[2048,256]{1,0:T(8,128)(2,1)} %constant_dynamic-slice_fusion), channel_id=1, source_target_pairs={{0,4},{4,0},{8,12},{12,8},{16,20},{20,16},{24,28},{28,24},{1,5},{5... | collective-permute-start | bytes 3145736 | tf_op jit(solution)/shard_map/ppermute | solution.py:232
  64.4 24.3 %collective-permute-start.3 = (f32[64]{0:T(128)S(1)}, f32[64]{0:T(128)S(1)}, u32[]{:S(2)}, u32[]{:S(2)}) collective-permute-start(f32[64]{0:T(128)S(1)} %exp.20), channel_id=1, source_target_pairs={{0,4},{4,0},{8,12},{12,8},{16,20},{20,16},{24,28},{28,24},{1,5},{5... | collective-permute-start | bytes 776 | tf_op jit(solution)/shard_map/ppermute | solution.py:232
  90.4 46.4 %collective-permute-start.5 = (bf16[2048,256]{1,0:T(8,128)(2,1)}, bf16[2048,256]{1,0:T(8,128)(2,1)}, u32[]{:S(2)}, u32[]{:S(2)}) collective-permute-start(bf16[2048,256]{1,0:T(8,128)(2,1)} %fusion.1), channel_id=1, source_target_pairs={{0,8},{4,12},{8,16},{12,20},{16,24},{20,28},{1,9},{5,13},{9,17},{1... | collective-permute-start | bytes 3145736 | tf_op jit(solution)/shard_map/ppermute | solution.py:236
  138.8 25.6 %collective-permute-start.6 = (bf16[2048,256]{1,0:T(8,128)(2,1)S(1)}, bf16[2048,256]{1,0:T(8,128)(2,1)S(1)}, u32[]{:S(2)}, u32[]{:S(2)}) collective-permute-start(bf16[2048,256]{1,0:T(8,128)(2,1)S(1)} %add_convert_fusion.9), channel_id=1, source_target_pairs={{0,8},{4,12},{8,16},{12,20},{16,24},{20,28},{1,9},{5,13},{9,17},{1... | collective-permute-start | bytes 3145736 | tf_op jit(solution)/shard_map/ppermute | solution.py:236
  164.5 1.7 copy-start.18
  164.5 9.0 %copy-start.21 = (f32[64,4,128]{2,1,0:T(4,128)S(1)}, f32[64,4,128]{2,1,0:T(4,128)}, u32[]{:S(2)}) copy-start(f32[64,4,128]{2,1,0:T(4,128)} %copy-done.20) | copy-start | bytes 393220
  164.5 10.1 %copy-start.27 = (bf16[4096]{0:T(1024)(128)(2,1)S(1)}, bf16[4096]{0:T(1024)(128)(2,1)}, u32[]{:S(2)}) copy-start(bf16[4096]{0:T(1024)(128)(2,1)} %param.25) | copy-start | bytes 24580
  164.6 10.1 %copy-start.23 = (f32[512]{0:T(512)S(1)}, f32[512]{0:T(512)}, u32[]{:S(2)}) copy-start(f32[512]{0:T(512)} %copy-done.22) | copy-start | bytes 6148
  166.2 23.1 %collective-permute-start.7 = (bf16[2048,256]{1,0:T(8,128)(2,1)}, bf16[2048,256]{1,0:T(8,128)(2,1)}, u32[]{:S(2)}, u32[]{:S(2)}) collective-permute-start(bf16[2048,256]{1,0:T(8,128)(2,1)} %broadcast_select_fusion.2), channel_id=1, source_target_pairs={{0,4},{4,0},{8,12},{12,8},{16,20},{20,16},{24,28},{28,24},{1,5},{5... | collective-permute-start | bytes 3145736 | tf_op jit(solution)/shard_map/ppermute | solution.py:232
  166.8 91.1 %collective-permute-start.14 = (bf16[4096,512]{1,0:T(8,128)(2,1)}, bf16[4096,512]{1,0:T(8,128)(2,1)}, u32[]{:S(2)}, u32[]{:S(2)}) collective-permute-start(bf16[4096,512]{1,0:T(8,128)(2,1)} %collective-permute-done.2.refs_5_), channel_id=1, source_target_pairs={{8,0},{12,4},{16,8},{20,12},{24,16},{28,20},{9,1},{13,5},{17,9},{2... | collective-permute-start | bytes 12582920 | tf_op jit(solution)/shard_map/ppermute | solution.py:236
  172.0 91.8 %collective-permute-start.10 = (bf16[4096,512]{1,0:T(8,128)(2,1)}, bf16[4096,512]{1,0:T(8,128)(2,1)}, u32[]{:S(2)}, u32[]{:S(2)}) collective-permute-start(bf16[4096,512]{1,0:T(8,128)(2,1)} %collective-permute-done.1.refs_4_), channel_id=1, source_target_pairs={{0,8},{4,12},{8,16},{12,20},{16,24},{20,28},{1,9},{5,13},{9,17},{1... | collective-permute-start | bytes 12582920 | tf_op jit(solution)/shard_map/ppermute | solution.py:236
  189.3 4.6 %copy-start.6 = (bf16[512,4096]{1,0:T(8,128)(2,1)S(1)}, bf16[512,4096]{1,0:T(8,128)(2,1)}, u32[]{:S(2)}) copy-start(bf16[512,4096]{1,0:T(8,128)(2,1)} %copy-done.5) | copy-start | bytes 12582916
  192.3 1.6 copy-start.10
  193.7 2.2 copy-start.4
  198.8 117.5 %copy-start = (bf16[512,2048]{1,0:T(8,128)(2,1)}, bf16[512,2048]{1,0:T(8,128)(2,1)S(1)}, u32[]{:S(2)}) copy-start(bf16[512,2048]{1,0:T(8,128)(2,1)S(1)} %gated_norm.2.refs_0_) | copy-start | bytes 6291460
  198.8 44.4 %collective-permute-start.8 = (bf16[512,2048]{1,0:T(8,128)(2,1)S(1)}, bf16[512,2048]{1,0:T(8,128)(2,1)S(1)}, u32[]{:S(2)}, u32[]{:S(2)}) collective-permute-start(bf16[512,2048]{1,0:T(8,128)(2,1)S(1)} %gated_norm.2.refs_0_), channel_id=1, source_target_pairs={{0,4},{4,0},{8,12},{12,8},{16,20},{20,16},{24,28},{28,24},{1,5},{5... | collective-permute-start | bytes 6291464 | tf_op jit(solution)/shard_map/ppermute | solution.py:232
  243.2 73.1 %copy-start.16 = (bf16[512,2048]{1,0:T(8,128)(2,1)}, bf16[512,2048]{1,0:T(8,128)(2,1)S(1)}, u32[]{:S(2)}) copy-start(bf16[512,2048]{1,0:T(8,128)(2,1)S(1)} %collective-permute-done.8.refs_2_) | copy-start | bytes 6291460
  265.1 90.9 %collective-permute-start.11 = (bf16[4096,512]{1,0:T(8,128)(2,1)}, bf16[4096,512]{1,0:T(8,128)(2,1)}, u32[]{:S(2)}, u32[]{:S(2)}) collective-permute-start(bf16[4096,512]{1,0:T(8,128)(2,1)} %get-tuple-element.26.refs_4_), channel_id=1, source_target_pairs={{0,8},{4,12},{8,16},{12,20},{16,24},{20,28},{1,9},{5,13},{9,17},{1... | collective-permute-start | bytes 12582920 | tf_op jit(solution)/shard_map/ppermute | solution.py:236
  266.4 101.5 %collective-permute-start.17 = (bf16[4096,512]{1,0:T(8,128)(2,1)}, bf16[4096,512]{1,0:T(8,128)(2,1)}, u32[]{:S(2)}, u32[]{:S(2)}) collective-permute-start(bf16[4096,512]{1,0:T(8,128)(2,1)} %get-tuple-element.25.refs_5_), channel_id=1, source_target_pairs={{8,0},{12,4},{16,8},{20,12},{24,16},{28,20},{9,1},{13,5},{17,9},{2... | collective-permute-start | bytes 12582920 | tf_op jit(solution)/shard_map/ppermute | solution.py:236
  273.0 43.2 %collective-permute-start.9 = (bf16[512,2048]{1,0:T(8,128)(2,1)S(1)}, bf16[512,2048]{1,0:T(8,128)(2,1)S(1)}, u32[]{:S(2)}, u32[]{:S(2)}) collective-permute-start(bf16[512,2048]{1,0:T(8,128)(2,1)S(1)} %gated_norm.3.refs_1_), channel_id=1, source_target_pairs={{0,4},{4,0},{8,12},{12,8},{16,20},{20,16},{24,28},{28,24},{1,5},{5... | collective-permute-start | bytes 6291464 | tf_op jit(solution)/shard_map/ppermute | solution.py:232
  316.2 1.3 copy-start.17
  325.8 53.3 %collective-permute-start.20 = (bf16[1024,512]{1,0:T(8,128)(2,1)S(1)}, bf16[1024,512]{1,0:T(8,128)(2,1)}, u32[]{:S(2)}, u32[]{:S(2)}) collective-permute-start(bf16[1024,512]{1,0:T(8,128)(2,1)S(1)} %project.7), channel_id=1, source_target_pairs={{1,0},{3,2},{5,4},{7,6},{8,9},{10,11},{12,13},{14,15},{17,16},{19,... | collective-permute-start | bytes 3145736 | tf_op jit(solution)/shard_map/ppermute | solution.py:410
  328.1 1.6 copy-start.1
  338.7 43.6 %collective-permute-start.15 = (bf16[1024,512]{1,0:T(8,128)(2,1)}, bf16[1024,512]{1,0:T(8,128)(2,1)}, u32[]{:S(2)}, u32[]{:S(2)}) collective-permute-start(bf16[1024,512]{1,0:T(8,128)(2,1)} %project.5), channel_id=1, source_target_pairs={{1,0},{3,2},{5,4},{7,6},{8,9},{10,11},{12,13},{14,15},{17,16},{19,... | collective-permute-start | bytes 3145736 | tf_op jit(solution)/shard_map/ppermute | solution.py:410
  356.1 1.6 copy-start.2
  366.6 19.2 %collective-permute-start.12 = (bf16[1024,512]{1,0:T(8,128)(2,1)}, bf16[1024,512]{1,0:T(8,128)(2,1)}, u32[]{:S(2)}, u32[]{:S(2)}) collective-permute-start(bf16[1024,512]{1,0:T(8,128)(2,1)} %project.4), channel_id=1, source_target_pairs={{0,1},{2,3},{4,5},{6,7},{9,8},{11,10},{13,12},{15,14},{16,17},{18,... | collective-permute-start | bytes 3145736 | tf_op jit(solution)/shard_map/ppermute | solution.py:410
  367.9 1.6 copy-start.3
  377.8 11.1 %collective-permute-start.18 = (bf16[1024,512]{1,0:T(8,128)(2,1)S(1)}, bf16[1024,512]{1,0:T(8,128)(2,1)S(1)}, u32[]{:S(2)}, u32[]{:S(2)}) collective-permute-start(bf16[1024,512]{1,0:T(8,128)(2,1)S(1)} %project.6), channel_id=1, source_target_pairs={{0,1},{2,3},{4,5},{6,7},{9,8},{11,10},{13,12},{15,14},{16,17},{18,... | collective-permute-start | bytes 3145736 | tf_op jit(solution)/shard_map/ppermute | solution.py:410
  380.6 16.1 %collective-permute-start.21 = (bf16[1024,512]{1,0:T(8,128)(2,1)S(1)}, bf16[1024,512]{1,0:T(8,128)(2,1)}, u32[]{:S(2)}, u32[]{:S(2)}) collective-permute-start(bf16[1024,512]{1,0:T(8,128)(2,1)S(1)} %add_convert_fusion.1), channel_id=1, source_target_pairs={{2,0},{6,4},{11,9},{15,13},{16,18},{20,22},{25,27},{29,31}} | collective-permute-start | bytes 3145736 | tf_op jit(solution)/shard_map/ppermute | solution.py:410
  384.1 12.5 %collective-permute-start.16 = (bf16[1024,512]{1,0:T(8,128)(2,1)S(1)}, bf16[1024,512]{1,0:T(8,128)(2,1)}, u32[]{:S(2)}, u32[]{:S(2)}) collective-permute-start(bf16[1024,512]{1,0:T(8,128)(2,1)S(1)} %add_convert_fusion.5), channel_id=1, source_target_pairs={{0,2},{4,6},{9,11},{13,15},{18,16},{22,20},{27,25},{31,29}} | collective-permute-start | bytes 3145736 | tf_op jit(solution)/shard_map/ppermute | solution.py:410
  387.6 27.8 %collective-permute-start.13 = (bf16[1024,512]{1,0:T(8,128)(2,1)S(1)}, bf16[1024,512]{1,0:T(8,128)(2,1)}, u32[]{:S(2)}, u32[]{:S(2)}) collective-permute-start(bf16[1024,512]{1,0:T(8,128)(2,1)S(1)} %add_convert_fusion.7), channel_id=1, source_target_pairs={{3,1},{7,5},{8,10},{12,14},{17,19},{21,23},{26,24},{30,28}} | collective-permute-start | bytes 3145736 | tf_op jit(solution)/shard_map/ppermute | solution.py:410
  390.2 25.3 %collective-permute-start.19 = (bf16[1024,512]{1,0:T(8,128)(2,1)}, bf16[1024,512]{1,0:T(8,128)(2,1)}, u32[]{:S(2)}, u32[]{:S(2)}) collective-permute-start(bf16[1024,512]{1,0:T(8,128)(2,1)} %add_convert_fusion.3), channel_id=1, source_target_pairs={{1,3},{5,7},{10,8},{14,12},{19,17},{23,21},{24,26},{28,30}} | collective-permute-start | bytes 3145736 | tf_op jit(solution)/shard_map/ppermute | solution.py:410
  419.1 14.0 %collective-permute-start.22 = (bf16[1,512,512]{2,1,0:T(8,128)(2,1)S(1)}, bf16[1,512,512]{2,1,0:T(8,128)(2,1)S(1)}, u32[]{:S(2)}, u32[]{:S(2)}) collective-permute-start(bf16[1,512,512]{2,1,0:T(8,128)(2,1)S(1)} %slice.79), channel_id=1, source_target_pairs={{0,4},{4,0},{8,12},{12,8},{16,20},{20,16},{24,28},{28,24},{1,5},{5... | collective-permute-start | bytes 1572872 | tf_op jit(solution)/shard_map/ppermute | solution.py:232
